TPU v7x, 32 devices: a whole 2x2x4 slice. The times are simulated.
32 devices in a mesh: leaf: 32 (over z, y, x, core).
Axes of the slice: x: 2, y: 2, z: 4, core: 2. Of those that a mesh axis runs over, the one named last changes fastest.
Arguments:
- density: bfloat16 [32768, 220], P('leaf'), may hold values from -6 to 6
- vel_mask: int32 [32768], P('leaf'), may hold values from 0 to 1, as said below
- near_list: int32 [32768, 27], P('leaf'), may hold values from 0 to 32767, as said below
- near_ops: bfloat16 [27, 220, 660], replicated, may hold values from -0.078125 to 0.078125
- upward_ops: bfloat16 [8, 220, 56], replicated, may hold values from -0.0068359375 to 0.0068359375
- coupling_operators: float32 [56, 168], replicated, may hold values from -0.75 to 0.75
- coarse_weights: float32 [8, 8], replicated, may hold values from -2 to 2
- downward_ops: bfloat16 [8, 56, 220], replicated, may hold values from -0.75 to 0.75
- conc_owner: int32 [32768, 1], P('leaf'), may hold values from 0 to 31; in each aligned block of 1024 rows (0 to 1023, 1024 to 2047, ...) at most 64 rows name the same one
- concentration: bfloat16 [65536, 220], P('leaf'), may hold values from -6 to 6
- departure: int32 [65536], P('leaf'), may hold values from 0 to 2047
- departure_class: int32 [65536], P('leaf'), may hold values from 0 to 7
- shift_ops: bfloat16 [8, 220, 220], replicated, may hold values from -0.4375 to 0.4375
- eval_ops: bfloat16 [220, 1024], replicated, may hold values from -0.4375 to 0.4375
Outputs:
- velocity: bfloat16 [32768, 660], P('leaf')
- advected: bfloat16 [65536, 256], P('leaf')
Inputs may be any that keep to these rules, and one draw needn't show every extreme that they name: `vel_mask`: in each aligned block of 1024 rows the real leaves come first; every block has from 341 to 1024 real leaves, and both counts occur in every draw. `near_list`: entry [i, t] lies within 1024 of i; column 13 is i itself. `conc_owner`: in each aligned block of 1024 rows, the rows of one device, no owner is named more than 64 times, a bound that some block reaches. `departure`: A slot index within the same device's 2048 slots.
All inputs are finite; a program needn't handle non-finite values.
Results may differ from a plain program's by a relative error of at most 0.008.
Values may be sent and summed in bfloat16 or wider, within the bound.
A program may use at most 128 MiB of HBM per device.

v0:
```python
import jax
import jax.numpy as jnp
from jax import lax
from jax.sharding import PartitionSpec as P

SPAN = 4


time_step = 0.5


def with_halo(block, sides, width):
    for axis, dim in sides:
        count = lax.axis_size(axis)
        forward = [(i, i + 1) for i in range(count - 1)]
        backward = [(target, source) for source, target in forward]
        low = lax.ppermute(
            lax.slice_in_dim(block, block.shape[dim] - width, None, axis=dim), axis, forward
        )
        high = lax.ppermute(lax.slice_in_dim(block, 0, width, axis=dim), axis, backward)
        block = jnp.concatenate([low, block, high], axis=dim)
    return block


def shifted_rows(gathered, classes, shift_ops):
    kinds = shift_ops.shape[0]
    total = jnp.zeros((gathered.shape[0], shift_ops.shape[2]), jnp.float32)
    for kind in range(kinds):
        product = jnp.dot(gathered, shift_ops[kind], preferred_element_type=jnp.float32)
        total = jnp.where((classes == kind)[:, None], product, total)
    return total.astype(jnp.bfloat16)


def advect_rows(base, velocity_rows, alive_rows, eval_ops):
    value_rows = jnp.dot(base, eval_ops, preferred_element_type=jnp.float32)
    nodes_count = value_rows.shape[1] // 4
    speeds = jnp.dot(
        velocity_rows.reshape(-1, eval_ops.shape[0]),
        eval_ops[:, :nodes_count],
        preferred_element_type=jnp.float32,
    )
    speeds = speeds.reshape(base.shape[0], 3, nodes_count)
    correction = speeds[:, 0] * value_rows[:, nodes_count : 2 * nodes_count]
    correction = correction + speeds[:, 1] * value_rows[:, 2 * nodes_count : 3 * nodes_count]
    correction = correction + speeds[:, 2] * value_rows[:, 3 * nodes_count :]
    return (alive_rows[:, None] * (value_rows[:, :nodes_count] - time_step * correction)).astype(
        jnp.bfloat16
    )


def local(
    density,
    vel_mask,
    near_list,
    near_ops,
    upward_ops,
    coupling_operators,
    coarse_weights,
    downward_ops,
    conc_owner,
    concentration,
    departure,
    departure_class,
    shift_ops,
    eval_ops,
):
    leaves = density.shape[0]
    coef_width = density.shape[1]
    devices = lax.axis_size("leaf")
    my_index = lax.axis_index("leaf")
    alive = vel_mask.astype(jnp.float32)
    live_density = (density.astype(jnp.float32) * alive[:, None]).astype(jnp.bfloat16)
    padded = with_halo(live_density, (("leaf", 0),), leaves)
    local_rows = near_list - my_index * leaves + leaves

    def near_step(position, total):
        rows = lax.dynamic_index_in_dim(local_rows, position, 1, keepdims=False)
        picked = jnp.take(padded, rows, axis=0)
        operator = lax.dynamic_index_in_dim(near_ops, position, 0, keepdims=False)
        return total + jnp.dot(picked, operator, preferred_element_type=jnp.float32)

    nearby_field = lax.fori_loop(
        0, near_ops.shape[0], near_step, jnp.zeros((leaves, 3 * coef_width), jnp.float32)
    )
    parts = jnp.einsum(
        "gop,opq->goq",
        live_density.reshape(-1, 8, coef_width),
        upward_ops,
        preferred_element_type=jnp.float32,
    )
    own_part = jnp.sum(parts, axis=(0, 1))
    boxes = devices // SPAN
    my_box = my_index // SPAN
    box_rows = (jnp.arange(boxes, dtype=jnp.int32) == my_box).astype(jnp.float32)
    moments = lax.psum(box_rows[:, None] * own_part[None, :], "leaf")
    expanded = jnp.dot(moments, coupling_operators, precision=lax.Precision.HIGHEST)
    weight_row = lax.dynamic_slice_in_dim(coarse_weights, my_box, 1, 0)
    own_expansion = jnp.dot(weight_row, expanded, precision=lax.Precision.HIGHEST)
    box_far = jnp.einsum(
        "jq,oqp->ojp",
        own_expansion.reshape(3, -1),
        downward_ops.astype(jnp.float32),
        precision=lax.Precision.HIGHEST,
    )
    far_field = jnp.broadcast_to(
        box_far.reshape(1, 8, 3 * coef_width), (leaves // 8, 8, 3 * coef_width)
    ).reshape(leaves, 3 * coef_width)
    velocity = ((nearby_field + far_field) * alive[:, None]).astype(jnp.bfloat16)
    slots_here = concentration.shape[0]
    capacity = slots_here // devices
    owner = conc_owner[:, 0]
    onehot = (owner[:, None] == jnp.arange(devices, dtype=jnp.int32)[None, :]).astype(jnp.int32)
    rank = jnp.sum(jnp.cumsum(onehot, axis=0) * onehot, axis=1) - 1
    send_slot = owner * capacity + rank
    placement = (jnp.arange(slots_here, dtype=jnp.int32)[:, None] == send_slot[None, :]).astype(
        jnp.bfloat16
    )
    send_velocity = jnp.dot(placement, velocity, preferred_element_type=jnp.float32).astype(
        jnp.bfloat16
    )
    send_alive = jnp.dot(
        placement, vel_mask.astype(jnp.bfloat16), preferred_element_type=jnp.float32
    ).astype(jnp.bfloat16)
    base = shifted_rows(concentration[departure], departure_class, shift_ops)
    got_base = lax.all_to_all(
        base.reshape(devices, capacity, -1), "leaf", split_axis=0, concat_axis=0, tiled=True
    )
    result = advect_rows(
        got_base.reshape(slots_here, -1), send_velocity, send_alive.astype(jnp.float32), eval_ops
    )
    returned = lax.all_to_all(
        result.reshape(devices, capacity, -1), "leaf", split_axis=0, concat_axis=0, tiled=True
    )
    advected = returned.reshape(slots_here, -1)
    return (velocity, advected)


def solution(mesh):
    placed = (
        P("leaf", None),
        P("leaf"),
        P("leaf", None),
        P(),
        P(),
        P(),
        P(),
        P(),
        P("leaf", None),
        P("leaf", None),
        P("leaf"),
        P("leaf"),
        P(),
        P(),
    )
    return jax.shard_map(
        local,
        mesh=mesh,
        in_specs=placed,
        out_specs=(P("leaf", None), P("leaf", None)),
        check_vma=False,
    )
```

profile of v0, /device:TPU:0, one launch (start us, length us, event | category | flops | bytes accessed | tf_op | source)
XLA Modules:
  0.0 359.9 jit_solution(12529718514493848174)
XLA Ops:
  13.4 7.5 %gather_fusion.1 = bf16[2048,220]{1,0:T(8,128)(2,1)S(1)} fusion(bf16[2048,220]{1,0:T(8,128)(2,1)S(1)} %copy.39, s32[2048]{0:T(1024)S(1)} %fusion.41), kind=kCustom, calls=%fused_computation.1 | custom fusion | bytes 1810432 | tf_op jit(solution)/shard_map/gather | solution.py:124
  29.2 8.1 %all-to-all-start = ((bf16[32,64,220]{2,1,0:T(8,128)(2,1)}), bf16[32,64,220]{2,1,0:T(8,128)(2,1)}, u32[]{:S(2)}, u32[]{:S(2)}) async-start(bf16[32,64,220]{2,1,0:T(8,128)(2,1)} %bitcast.22), calls=%async_computation | async-start | bytes 2097152 | tf_op jit(solution)/shard_map/all_to_all | solution.py:125
  37.6 9.0 %reduce-window.6 = s32[32,8,128]{2,1,0:T(8,128)S(1)} reduce-window(s32[32,8,128]{2,1,0:T(8,128)S(1)} %fusion.30, s32[]{:T(128)} %constant.95.clone.1), window={size=1x1x128 pad=0_0x0_0x127_0}, to_apply=%region_4.5 | reduce-window | flops 4161536 | bytes 262148 | tf_op jit(solution)/shard_map/reduce-window
  47.6 40.7 %psum.7 = f32[8,56]{1,0:T(8,128)S(1)} all-reduce(f32[8,56]{1,0:T(8,128)S(1)} %broadcast_multiply_fusion), channel_id=1, replica_groups=mesh['leaf'=32] {'leaf'}, use_global_device_ids=true, to_apply=%region_3.4 | all-reduce | flops 448 | bytes 3584 | tf_op jit(solution)/shard_map/psum | solution.py:95
  92.6 216.7 %while.14 = (s32[]{:T(128)}, f32[1024,660]{0,1:T(8,128)}, s32[1024,27]{0,1:T(8,128)S(1)}, bf16[3072,220]{1,0:T(8,128)(2,1)S(1)}, bf16[27,220,660]{1,2,0:T(8,128)(2,1)}, /*index=5*/s32[]{:T(128)}, s32[]{:T(128)}) while((s32[]{:T(128)}, f32[1024,660]{0,1:T(8,128)}, s32[1024,27]{0,1:T(8,128)S(1)}, bf16[3072,220]{1,0:T(8,128)(2,1)S(1)}, ...), condition=%wide.region_1.2_spmd.clone, body=%wide.region_0.1_spmd.clone.sunk | while | flops 298953728 | bytes 7137383 | solution.py:82
  111.8 4.1 %select_add_fusion.2 = f32[1024,660]{0,1:T(8,128)} fusion(f32[1024,660]{0,1:T(8,128)} %get-tuple-element.192, pred[]{:T(512)S(6)} %compare.5, bf16[1024,220]{1,0:T(8,128)(2,1)S(1)} %gather_fusion, pred[1024]{0:T(1024)(128)(4,1)S(1)} %get-tuple-element.183, bf16[27,220,660]{1,2,0:T(8,128)(2,1)} %get-tuple-element.202, s32[]{:T(128)S(6)} %copy.88), kind=kOutput, calls=%fused_computation.2.clone.1 | convolution fusion | flops 298946560 | bytes 6214661 | tf_op jit(solution)/shard_map/while/body/eval_jaxpr/dot_general | solution.py:80
  119.9 4.1 %select_add_fusion.2 = f32[1024,660]{0,1:T(8,128)} fusion(f32[1024,660]{0,1:T(8,128)} %get-tuple-element.192, pred[]{:T(512)S(6)} %compare.5, bf16[1024,220]{1,0:T(8,128)(2,1)S(1)} %gather_fusion, pred[1024]{0:T(1024)(128)(4,1)S(1)} %get-tuple-element.183, bf16[27,220,660]{1,2,0:T(8,128)(2,1)} %get-tuple-element.202, s32[]{:T(128)S(6)} %copy.88), kind=kOutput, calls=%fused_computation.2.clone.1 | convolution fusion | flops 298946560 | bytes 6214661 | tf_op jit(solution)/shard_map/while/body/eval_jaxpr/dot_general | solution.py:80
  136.0 4.1 %select_add_fusion.2 = f32[1024,660]{0,1:T(8,128)} fusion(f32[1024,660]{0,1:T(8,128)} %get-tuple-element.192, pred[]{:T(512)S(6)} %compare.5, bf16[1024,220]{1,0:T(8,128)(2,1)S(1)} %gather_fusion, pred[1024]{0:T(1024)(128)(4,1)S(1)} %get-tuple-element.183, bf16[27,220,660]{1,2,0:T(8,128)(2,1)} %get-tuple-element.202, s32[]{:T(128)S(6)} %copy.88), kind=kOutput, calls=%fused_computation.2.clone.1 | convolution fusion | flops 298946560 | bytes 6214661 | tf_op jit(solution)/shard_map/while/body/eval_jaxpr/dot_general | solution.py:80
  152.1 4.1 %select_add_fusion.2 = f32[1024,660]{0,1:T(8,128)} fusion(f32[1024,660]{0,1:T(8,128)} %get-tuple-element.192, pred[]{:T(512)S(6)} %compare.5, bf16[1024,220]{1,0:T(8,128)(2,1)S(1)} %gather_fusion, pred[1024]{0:T(1024)(128)(4,1)S(1)} %get-tuple-element.183, bf16[27,220,660]{1,2,0:T(8,128)(2,1)} %get-tuple-element.202, s32[]{:T(128)S(6)} %copy.88), kind=kOutput, calls=%fused_computation.2.clone.1 | convolution fusion | flops 298946560 | bytes 6214661 | tf_op jit(solution)/shard_map/while/body/eval_jaxpr/dot_general | solution.py:80
  160.2 4.1 %select_add_fusion.2 = f32[1024,660]{0,1:T(8,128)} fusion(f32[1024,660]{0,1:T(8,128)} %get-tuple-element.192, pred[]{:T(512)S(6)} %compare.5, bf16[1024,220]{1,0:T(8,128)(2,1)S(1)} %gather_fusion, pred[1024]{0:T(1024)(128)(4,1)S(1)} %get-tuple-element.183, bf16[27,220,660]{1,2,0:T(8,128)(2,1)} %get-tuple-element.202, s32[]{:T(128)S(6)} %copy.88), kind=kOutput, calls=%fused_computation.2.clone.1 | convolution fusion | flops 298946560 | bytes 6214661 | tf_op jit(solution)/shard_map/while/body/eval_jaxpr/dot_general | solution.py:80
  176.3 4.1 %select_add_fusion.2 = f32[1024,660]{0,1:T(8,128)} fusion(f32[1024,660]{0,1:T(8,128)} %get-tuple-element.192, pred[]{:T(512)S(6)} %compare.5, bf16[1024,220]{1,0:T(8,128)(2,1)S(1)} %gather_fusion, pred[1024]{0:T(1024)(128)(4,1)S(1)} %get-tuple-element.183, bf16[27,220,660]{1,2,0:T(8,128)(2,1)} %get-tuple-element.202, s32[]{:T(128)S(6)} %copy.88), kind=kOutput, calls=%fused_computation.2.clone.1 | convolution fusion | flops 298946560 | bytes 6214661 | tf_op jit(solution)/shard_map/while/body/eval_jaxpr/dot_general | solution.py:80
  184.4 4.1 %select_add_fusion.2 = f32[1024,660]{0,1:T(8,128)} fusion(f32[1024,660]{0,1:T(8,128)} %get-tuple-element.192, pred[]{:T(512)S(6)} %compare.5, bf16[1024,220]{1,0:T(8,128)(2,1)S(1)} %gather_fusion, pred[1024]{0:T(1024)(128)(4,1)S(1)} %get-tuple-element.183, bf16[27,220,660]{1,2,0:T(8,128)(2,1)} %get-tuple-element.202, s32[]{:T(128)S(6)} %copy.88), kind=kOutput, calls=%fused_computation.2.clone.1 | convolution fusion | flops 298946560 | bytes 6214661 | tf_op jit(solution)/shard_map/while/body/eval_jaxpr/dot_general | solution.py:80
  200.5 4.1 %select_add_fusion.2 = f32[1024,660]{0,1:T(8,128)} fusion(f32[1024,660]{0,1:T(8,128)} %get-tuple-element.192, pred[]{:T(512)S(6)} %compare.5, bf16[1024,220]{1,0:T(8,128)(2,1)S(1)} %gather_fusion, pred[1024]{0:T(1024)(128)(4,1)S(1)} %get-tuple-element.183, bf16[27,220,660]{1,2,0:T(8,128)(2,1)} %get-tuple-element.202, s32[]{:T(128)S(6)} %copy.88), kind=kOutput, calls=%fused_computation.2.clone.1 | convolution fusion | flops 298946560 | bytes 6214661 | tf_op jit(solution)/shard_map/while/body/eval_jaxpr/dot_general | solution.py:80
  216.6 4.1 %select_add_fusion.2 = f32[1024,660]{0,1:T(8,128)} fusion(f32[1024,660]{0,1:T(8,128)} %get-tuple-element.192, pred[]{:T(512)S(6)} %compare.5, bf16[1024,220]{1,0:T(8,128)(2,1)S(1)} %gather_fusion, pred[1024]{0:T(1024)(128)(4,1)S(1)} %get-tuple-element.183, bf16[27,220,660]{1,2,0:T(8,128)(2,1)} %get-tuple-element.202, s32[]{:T(128)S(6)} %copy.88), kind=kOutput, calls=%fused_computation.2.clone.1 | convolution fusion | flops 298946560 | bytes 6214661 | tf_op jit(solution)/shard_map/while/body/eval_jaxpr/dot_general | solution.py:80
  224.7 4.1 %select_add_fusion.2 = f32[1024,660]{0,1:T(8,128)} fusion(f32[1024,660]{0,1:T(8,128)} %get-tuple-element.192, pred[]{:T(512)S(6)} %compare.5, bf16[1024,220]{1,0:T(8,128)(2,1)S(1)} %gather_fusion, pred[1024]{0:T(1024)(128)(4,1)S(1)} %get-tuple-element.183, bf16[27,220,660]{1,2,0:T(8,128)(2,1)} %get-tuple-element.202, s32[]{:T(128)S(6)} %copy.88), kind=kOutput, calls=%fused_computation.2.clone.1 | convolution fusion | flops 298946560 | bytes 6214661 | tf_op jit(solution)/shard_map/while/body/eval_jaxpr/dot_general | solution.py:80
  240.8 4.1 %select_add_fusion.2 = f32[1024,660]{0,1:T(8,128)} fusion(f32[1024,660]{0,1:T(8,128)} %get-tuple-element.192, pred[]{:T(512)S(6)} %compare.5, bf16[1024,220]{1,0:T(8,128)(2,1)S(1)} %gather_fusion, pred[1024]{0:T(1024)(128)(4,1)S(1)} %get-tuple-element.183, bf16[27,220,660]{1,2,0:T(8,128)(2,1)} %get-tuple-element.202, s32[]{:T(128)S(6)} %copy.88), kind=kOutput, calls=%fused_computation.2.clone.1 | convolution fusion | flops 298946560 | bytes 6214661 | tf_op jit(solution)/shard_map/while/body/eval_jaxpr/dot_general | solution.py:80
  248.8 4.1 %select_add_fusion.2 = f32[1024,660]{0,1:T(8,128)} fusion(f32[1024,660]{0,1:T(8,128)} %get-tuple-element.192, pred[]{:T(512)S(6)} %compare.5, bf16[1024,220]{1,0:T(8,128)(2,1)S(1)} %gather_fusion, pred[1024]{0:T(1024)(128)(4,1)S(1)} %get-tuple-element.183, bf16[27,220,660]{1,2,0:T(8,128)(2,1)} %get-tuple-element.202, s32[]{:T(128)S(6)} %copy.88), kind=kOutput, calls=%fused_computation.2.clone.1 | convolution fusion | flops 298946560 | bytes 6214661 | tf_op jit(solution)/shard_map/while/body/eval_jaxpr/dot_general | solution.py:80
  264.9 4.1 %select_add_fusion.2 = f32[1024,660]{0,1:T(8,128)} fusion(f32[1024,660]{0,1:T(8,128)} %get-tuple-element.192, pred[]{:T(512)S(6)} %compare.5, bf16[1024,220]{1,0:T(8,128)(2,1)S(1)} %gather_fusion, pred[1024]{0:T(1024)(128)(4,1)S(1)} %get-tuple-element.183, bf16[27,220,660]{1,2,0:T(8,128)(2,1)} %get-tuple-element.202, s32[]{:T(128)S(6)} %copy.88), kind=kOutput, calls=%fused_computation.2.clone.1 | convolution fusion | flops 298946560 | bytes 6214661 | tf_op jit(solution)/shard_map/while/body/eval_jaxpr/dot_general | solution.py:80
  281.1 4.1 %select_add_fusion.2 = f32[1024,660]{0,1:T(8,128)} fusion(f32[1024,660]{0,1:T(8,128)} %get-tuple-element.192, pred[]{:T(512)S(6)} %compare.5, bf16[1024,220]{1,0:T(8,128)(2,1)S(1)} %gather_fusion, pred[1024]{0:T(1024)(128)(4,1)S(1)} %get-tuple-element.183, bf16[27,220,660]{1,2,0:T(8,128)(2,1)} %get-tuple-element.202, s32[]{:T(128)S(6)} %copy.88), kind=kOutput, calls=%fused_computation.2.clone.1 | convolution fusion | flops 298946560 | bytes 6214661 | tf_op jit(solution)/shard_map/while/body/eval_jaxpr/dot_general | solution.py:80
  289.1 4.1 %select_add_fusion.2 = f32[1024,660]{0,1:T(8,128)} fusion(f32[1024,660]{0,1:T(8,128)} %get-tuple-element.192, pred[]{:T(512)S(6)} %compare.5, bf16[1024,220]{1,0:T(8,128)(2,1)S(1)} %gather_fusion, pred[1024]{0:T(1024)(128)(4,1)S(1)} %get-tuple-element.183, bf16[27,220,660]{1,2,0:T(8,128)(2,1)} %get-tuple-element.202, s32[]{:T(128)S(6)} %copy.88), kind=kOutput, calls=%fused_computation.2.clone.1 | convolution fusion | flops 298946560 | bytes 6214661 | tf_op jit(solution)/shard_map/while/body/eval_jaxpr/dot_general | solution.py:80
  305.2 4.1 %select_add_fusion.2 = f32[1024,660]{0,1:T(8,128)} fusion(f32[1024,660]{0,1:T(8,128)} %get-tuple-element.192, pred[]{:T(512)S(6)} %compare.5, bf16[1024,220]{1,0:T(8,128)(2,1)S(1)} %gather_fusion, pred[1024]{0:T(1024)(128)(4,1)S(1)} %get-tuple-element.183, bf16[27,220,660]{1,2,0:T(8,128)(2,1)} %get-tuple-element.202, s32[]{:T(128)S(6)} %copy.88), kind=kOutput, calls=%fused_computation.2.clone.1 | convolution fusion | flops 298946560 | bytes 6214661 | tf_op jit(solution)/shard_map/while/body/eval_jaxpr/dot_general | solution.py:80
  313.1 4.5 %fusion.11 = bf16[2048,660]{0,1:T(8,128)(2,1)} fusion(bf16[1024,660]{1,0:T(8,128)(2,1)S(1)} %fusion.13, s32[1024]{0:T(1024)S(1)} %add_add_fusion), kind=kOutput, calls=%fused_computation.18 | convolution fusion | flops 2771689472 | bytes 4059136 | tf_op jit(solution)/shard_map/dot_general | solution.py:118
  328.2 4.5 %all-to-all-start.1 = ((bf16[32,64,256]{2,1,0:T(8,128)(2,1)}), bf16[32,64,256]{2,1,0:T(8,128)(2,1)S(1)}, u32[]{:S(2)}, u32[]{:S(2)}) async-start(bf16[32,64,256]{2,1,0:T(8,128)(2,1)} %bitcast.28), calls=%async_computation.1 | async-start | bytes 2097152 | tf_op jit(solution)/shard_map/all_to_all | solution.py:131
  334.1 24.7 %all-to-all-done.1 = bf16[32,64,256]{2,1,0:T(8,128)(2,1)S(1)} async-done(((bf16[32,64,256]{2,1,0:T(8,128)(2,1)}), bf16[32,64,256]{2,1,0:T(8,128)(2,1)S(1)}, u32[]{:S(2)}, u32[]{:S(2)}) %all-to-all-start.1) | async-done | bytes 1048608 | tf_op jit(solution)/shard_map/all_to_all | solution.py:131
  (177 shorter events, 194.3 us)
Async XLA Ops:
  0.6 88.7 %copy-start = (bf16[8,56,220]{2,1,0:T(8,128)(2,1)S(1)}, bf16[8,56,220]{2,1,0:T(8,128)(2,1)}, u32[]{:S(2)}) copy-start(bf16[8,56,220]{2,1,0:T(8,128)(2,1)} %param.23) | copy-start | bytes 591364
  0.6 10.3 %copy-start.4 = (bf16[8,220,220]{2,0,1:T(8,128)(2,1)S(1)}, bf16[8,220,220]{2,0,1:T(8,128)(2,1)}, u32[]{:S(2)}) copy-start(bf16[8,220,220]{2,0,1:T(8,128)(2,1)} %param.28) | copy-start | bytes 2323204
  2.9 88.2 %collective-permute-start.1 = (bf16[1024,220]{1,0:T(8,128)(2,1)S(1)}, bf16[1024,220]{1,0:T(8,128)(2,1)}, u32[]{:S(2)}, u32[]{:S(2)}) collective-permute-start(bf16[1024,220]{1,0:T(8,128)(2,1)S(1)} %multiply_convert_fusion), channel_id=1, source_target_pairs={{1,0},{2,1},{3,2},{4,3},{5,4},{6,5},{7,6},{8,7},{9,8},{10,9},{11,1... | collective-permute-start | bytes 1351688 | tf_op jit(solution)/shard_map/ppermute | solution.py:20
  4.2 87.0 %collective-permute-start = (bf16[1024,220]{1,0:T(8,128)(2,1)S(1)}, bf16[1024,220]{1,0:T(8,128)(2,1)}, u32[]{:S(2)}, u32[]{:S(2)}) collective-permute-start(bf16[1024,220]{1,0:T(8,128)(2,1)S(1)} %multiply_convert_fusion), channel_id=1, source_target_pairs={{0,1},{1,2},{2,3},{3,4},{4,5},{5,6},{6,7},{7,8},{8,9},{9,10},{10,1... | collective-permute-start | bytes 1351688 | tf_op jit(solution)/shard_map/ppermute | solution.py:17
  20.9 3.0 copy-start.9
  20.9 3.6 copy-start.8
  22.5 2.6 copy-start.7
  24.0 1.6 copy-start.11
  25.6 0.9 copy-start.10
  26.2 1.0 copy-start.6
  27.8 9.7 %copy-start.14 = (s32[1024,1]{0,1:T(1,128)S(1)}, s32[1024,1]{0,1:T(1,128)}, u32[]{:S(2)}) copy-start(s32[1024,1]{0,1:T(1,128)} %param.24) | copy-start | bytes 12292
  29.2 17.9 %copy-start.15 = (bf16[8,220,56]{1,2,0:T(8,128)(2,1)S(1)}, bf16[8,220,56]{1,2,0:T(8,128)(2,1)}, u32[]{:S(2)}) copy-start(bf16[8,220,56]{1,2,0:T(8,128)(2,1)} %param.20) | copy-start | bytes 591364
  29.2 59.1 %copy-start.13 = (f32[56,168]{1,0:T(8,128)S(1)}, f32[56,168]{1,0:T(8,128)}, u32[]{:S(2)}) copy-start(f32[56,168]{1,0:T(8,128)} %param.21) | copy-start | bytes 112900
  29.2 294.2 %all-to-all-start = ((bf16[32,64,220]{2,1,0:T(8,128)(2,1)}), bf16[32,64,220]{2,1,0:T(8,128)(2,1)}, u32[]{:S(2)}, u32[]{:S(2)}) async-start(bf16[32,64,220]{2,1,0:T(8,128)(2,1)} %bitcast.22), calls=%async_computation | async-start | bytes 2097152 | tf_op jit(solution)/shard_map/all_to_all | solution.py:125
  46.8 44.3 %copy-start.12 = (s32[1024,27]{0,1:T(8,128)S(1)}, s32[1024,27]{0,1:T(8,128)}, u32[]{:S(2)}) copy-start(s32[1024,27]{0,1:T(8,128)} %param.18) | copy-start | bytes 331780
  311.9 1.2 copy-start.2
  317.6 2.0 copy-start.5
  323.3 3.1 copy-start.1
  328.1 4.5 %copy-start.3 = (bf16[1024,660]{1,0:T(8,128)(2,1)S(1)}, bf16[1024,660]{1,0:T(8,128)(2,1)}, u32[]{:S(2)}) copy-start(bf16[1024,660]{1,0:T(8,128)(2,1)} %copy-done.2) | copy-start | bytes 4055044
  328.2 30.7 %all-to-all-start.1 = ((bf16[32,64,256]{2,1,0:T(8,128)(2,1)}), bf16[32,64,256]{2,1,0:T(8,128)(2,1)S(1)}, u32[]{:S(2)}, u32[]{:S(2)}) async-start(bf16[32,64,256]{2,1,0:T(8,128)(2,1)} %bitcast.28), calls=%async_computation.1 | async-start | bytes 2097152 | tf_op jit(solution)/shard_map/all_to_all | solution.py:131
where the time goes:
time: 361 us; the launch traced here: 360 us
  local copies, waits for them, and re-layouts  130 us (36%)
  matrix products  129 us (36%)
  blocking collectives  40.7 us (11%)
  waiting for transfers between devices  24.7 us (7%)
  starting transfers between devices  17.7 us (5%)
  other arithmetic  16.4 us (5%)
    dot_general x27, matrix products, near_step(): return total + jnp.dot(picked, operator, preferred_element_type=jnp.float32)  109 us
    gather x27, local copies, waits for them, and re-layouts, near_step(): picked = jnp.take(padded, rows, axis=0)  106 us
    psum x1, blocking collectives, local(): moments = lax.psum(box_rows[:, None] * own_part[None, :], 'leaf')  40.7 us
    all_to_all x1, waiting for transfers between devices, local(): lax.all_to_all(result.reshape(devices, capacity, -1), 'leaf', split_axis=...  24.7 us
    another operation x3, other arithmetic  9.14 us
    all_to_all x1, starting transfers between devices, local(): lax.all_to_all(base.reshape(devices, capacity, -1), 'leaf', split_axis=0,...  8.1 us
    gather x1, local copies, waits for them, and re-layouts, local(): base = shifted_rows(concentration[departure], departure_class, shift_ops)  7.49 us
  transfers between devices with their start and end apart: 4, of which 1 were waited for; matrix products, arithmetic and copies ran while one was open for 74% of the time, Pallas kernels for 0%

commit v1 on v0

--- a/solution.py
+++ b/solution.py
@@ -1,6 +1,10 @@
+import functools
+
 import jax
 import jax.numpy as jnp
 from jax import lax
+from jax.experimental import pallas as pl
+from jax.experimental.pallas import tpu as pltpu
 from jax.sharding import PartitionSpec as P
 
 SPAN = 4
@@ -9,17 +13,104 @@
 time_step = 0.5
 
 
-def with_halo(block, sides, width):
-    for axis, dim in sides:
-        count = lax.axis_size(axis)
-        forward = [(i, i + 1) for i in range(count - 1)]
-        backward = [(target, source) for source, target in forward]
-        low = lax.ppermute(
-            lax.slice_in_dim(block, block.shape[dim] - width, None, axis=dim), axis, forward
-        )
-        high = lax.ppermute(lax.slice_in_dim(block, 0, width, axis=dim), axis, backward)
-        block = jnp.concatenate([low, block, high], axis=dim)
-    return block
+LANES = 128
+
+
+def halo(block):
+    count = lax.axis_size("leaf")
+    forward = [(i, i + 1) for i in range(count - 1)]
+    backward = [(target, source) for source, target in forward]
+    return lax.ppermute(block, "leaf", forward), lax.ppermute(block, "leaf", backward)
+
+
+def near_kernel(rows, group, idx_ref, low_ref, mid_ref, high_ref, ops_ref, out_ref, source, picked, lhs, weights):
+    block = pl.program_id(0)
+    taps, depth, _ = ops_ref.shape
+    wide = 2 * LANES
+    leaves = mid_ref.shape[0]
+
+    @pl.when(block == 0)
+    def _():
+        for part, ref in enumerate((low_ref, mid_ref, high_ref)):
+            @pl.loop(0, leaves // rows)
+            def _(chunk):
+                values = ref[pl.ds(chunk * rows, rows), :].astype(jnp.float32)
+                at = 2 * (part * leaves + chunk * rows)
+                source[pl.ds(at, rows, stride=2), :] = values[:, :LANES]
+                source[pl.ds(at + 1, rows, stride=2), :] = values[:, LANES:]
+
+        @pl.loop(0, taps)
+        def _(tap):
+            at = pl.multiple_of(tap * wide, wide)
+            weights[pl.ds(at, wide), :] = jnp.concatenate(
+                [ops_ref[tap], jnp.zeros((wide - depth, ops_ref.shape[2]), ops_ref.dtype)], axis=0
+            )
+
+    count = group * rows
+
+    def pick(turn):
+        at = (block * (taps // group) + turn) * count
+        for r in range(count):
+            row = pl.multiple_of(idx_ref[at + r], 2)
+            picked[pl.ds(2 * r, 2), :] = source[pl.ds(row, 2), :]
+
+    def settle():
+        for j in range(group):
+            for half in range(2):
+                values = picked[pl.ds(2 * j * rows + half, rows, stride=2), :]
+                lhs[:, (2 * j + half) * LANES : (2 * j + half + 1) * LANES] = values.astype(jnp.bfloat16)
+
+    def product(turn):
+        at = pl.multiple_of(turn * (group * wide), group * wide)
+        return jnp.dot(lhs[...], weights[pl.ds(at, group * wide), :], preferred_element_type=jnp.float32)
+
+    out_ref[...] = jnp.zeros_like(out_ref)
+    pick(0)
+    settle()
+
+    @pl.loop(0, taps // group - 1)
+    def _(turn):
+        out_ref[...] += product(turn)
+        pick(turn + 1)
+        settle()
+
+    out_ref[...] += product(taps // group - 1)
+
+
+def near_field(low, mid, high, local_rows, near_ops):
+    leaves = mid.shape[0]
+    taps, _, outs = near_ops.shape
+    rows = 256 if leaves % 256 == 0 else leaves
+    group = 3 if taps % 3 == 0 else 1
+    flat = (2 * local_rows).reshape(leaves // rows, rows, taps).transpose(0, 2, 1).reshape(-1)
+    vmem = pl.BlockSpec(memory_space=pltpu.VMEM)
+    return pl.pallas_call(
+        functools.partial(near_kernel, rows, group),
+        out_shape=jax.ShapeDtypeStruct((leaves, outs), jnp.float32),
+        grid=(leaves // rows,),
+        in_specs=[pl.BlockSpec(memory_space=pltpu.SMEM), vmem, vmem, vmem, vmem],
+        out_specs=pl.BlockSpec((rows, outs), lambda i: (i, 0)),
+        scratch_shapes=[
+            pltpu.VMEM((6 * leaves, LANES), jnp.float32),
+            pltpu.VMEM((2 * group * rows, LANES), jnp.float32),
+            pltpu.VMEM((rows, group * 2 * LANES), jnp.bfloat16),
+            pltpu.VMEM((taps * 2 * LANES, outs), jnp.bfloat16),
+        ],
+        compiler_params=pltpu.CompilerParams(
+            dimension_semantics=("arbitrary",), vmem_limit_bytes=48 * 1024 * 1024
+        ),
+        cost_estimate=pl.CostEstimate(
+            flops=2 * leaves * taps * 2 * LANES * outs * 5, bytes_accessed=100_000_000, transcendentals=0
+        ),
+        name="near_field",
+    )(flat, low, mid, high, near_ops)
+
+
+def split3(values):
+    high = values.astype(jnp.bfloat16)
+    rest = values - high.astype(jnp.float32)
+    middle = rest.astype(jnp.bfloat16)
+    return jnp.stack([high, middle, (rest - middle.astype(jnp.float32)).astype(jnp.bfloat16)], axis=-1)
 
 
 def shifted_rows(gathered, classes, shift_ops):
@@ -70,18 +161,10 @@
     my_index = lax.axis_index("leaf")
     alive = vel_mask.astype(jnp.float32)
     live_density = (density.astype(jnp.float32) * alive[:, None]).astype(jnp.bfloat16)
-    padded = with_halo(live_density, (("leaf", 0),), leaves)
+    wide = jnp.pad(live_density, ((0, 0), (0, 2 * LANES - coef_width)))
+    low, high = halo(wide)
     local_rows = near_list - my_index * leaves + leaves
-
-    def near_step(position, total):
-        rows = lax.dynamic_index_in_dim(local_rows, position, 1, keepdims=False)
-        picked = jnp.take(padded, rows, axis=0)
-        operator = lax.dynamic_index_in_dim(near_ops, position, 0, keepdims=False)
-        return total + jnp.dot(picked, operator, preferred_element_type=jnp.float32)
-
-    nearby_field = lax.fori_loop(
-        0, near_ops.shape[0], near_step, jnp.zeros((leaves, 3 * coef_width), jnp.float32)
-    )
+    nearby_field = near_field(low, wide, high, local_rows, near_ops)
     parts = jnp.einsum(
         "gop,opq->goq",
         live_density.reshape(-1, 8, coef_width),
@@ -89,10 +172,28 @@
         preferred_element_type=jnp.float32,
     )
     own_part = jnp.sum(parts, axis=(0, 1))
-    boxes = devices // SPAN
+    slots_here = concentration.shape[0]
+    capacity = slots_here // devices
+    base = shifted_rows(concentration[departure], departure_class, shift_ops)
+    densities = own_part.shape[0]
+    columns = -(-densities // capacity)
+    carried = split3(jnp.pad(own_part, (0, columns * capacity - densities)))
+    carried = jnp.broadcast_to(
+        carried.reshape(1, capacity, 3 * columns), (devices, capacity, 3 * columns)
+    )
+    got = lax.all_to_all(
+        jnp.concatenate([base.reshape(devices, capacity, coef_width), carried], axis=2),
+        "leaf",
+        split_axis=0,
+        concat_axis=0,
+        tiled=True,
+    )
+    got_base = got[:, :, :coef_width]
+    all_parts = jnp.sum(
+        got[:, :, coef_width:].astype(jnp.float32).reshape(devices, columns * capacity, 3), axis=2
+    )[:, :densities]
+    moments = jnp.sum(all_parts.reshape(devices // SPAN, SPAN, densities), axis=1)
     my_box = my_index // SPAN
-    box_rows = (jnp.arange(boxes, dtype=jnp.int32) == my_box).astype(jnp.float32)
-    moments = lax.psum(box_rows[:, None] * own_part[None, :], "leaf")
     expanded = jnp.dot(moments, coupling_operators, precision=lax.Precision.HIGHEST)
     weight_row = lax.dynamic_slice_in_dim(coarse_weights, my_box, 1, 0)
     own_expansion = jnp.dot(weight_row, expanded, precision=lax.Precision.HIGHEST)
@@ -106,11 +207,12 @@
         box_far.reshape(1, 8, 3 * coef_width), (leaves // 8, 8, 3 * coef_width)
     ).reshape(leaves, 3 * coef_width)
     velocity = ((nearby_field + far_field) * alive[:, None]).astype(jnp.bfloat16)
-    slots_here = concentration.shape[0]
-    capacity = slots_here // devices
     owner = conc_owner[:, 0]
-    onehot = (owner[:, None] == jnp.arange(devices, dtype=jnp.int32)[None, :]).astype(jnp.int32)
-    rank = jnp.sum(jnp.cumsum(onehot, axis=0) * onehot, axis=1) - 1
+    onehot = owner[:, None] == jnp.arange(devices, dtype=jnp.int32)[None, :]
+    order = jnp.arange(leaves, dtype=jnp.int32)
+    earlier = (order[None, :] < order[:, None]).astype(jnp.bfloat16)
+    before = jnp.dot(earlier, onehot.astype(jnp.bfloat16), preferred_element_type=jnp.float32)
+    rank = jnp.sum(jnp.where(onehot, before, 0.0), axis=1).astype(jnp.int32)
     send_slot = owner * capacity + rank
     placement = (jnp.arange(slots_here, dtype=jnp.int32)[:, None] == send_slot[None, :]).astype(
         jnp.bfloat16
@@ -121,10 +223,6 @@
     send_alive = jnp.dot(
         placement, vel_mask.astype(jnp.bfloat16), preferred_element_type=jnp.float32
     ).astype(jnp.bfloat16)
-    base = shifted_rows(concentration[departure], departure_class, shift_ops)
-    got_base = lax.all_to_all(
-        base.reshape(devices, capacity, -1), "leaf", split_axis=0, concat_axis=0, tiled=True
-    )
     result = advect_rows(
         got_base.reshape(slots_here, -1), send_velocity, send_alive.astype(jnp.float32), eval_ops
     )

time: 361 us -> 154 us (0.43)
  matrix products: 129 us -> 19.3 us
  local copies, waits for them, and re-layouts: 130 us -> 44.3 us
  blocking collectives: 40.7 us -> 0 us
  Pallas kernels: 0 us -> 38.6 us
  other arithmetic: 16.4 us -> 6.19 us
    dot_general x27 -> x1, matrix products: 109 us -> 0.54 us  [local(): jnp.dot(earlier, onehot.astype(jnp.bfloat16), preferred_element_type=jnp....]
    gather x27 -> x0, local copies, waits for them, and re-layouts: 106 us -> none  [near_step(): picked = jnp.take(padded, rows, axis=0)]
    psum x1 -> x0, blocking collectives: 40.7 us -> none  [local(): moments = lax.psum(box_rows[:, None] * own_part[None, :], 'leaf')]
    pallas_call x0 -> x1, Pallas kernels: none -> 38.6 us  [near_field(): pl.pallas_call(functools.partial(near_kernel, rows, group), out_shape=jax...]
    unnamed x36 -> x45, local copies, waits for them, and re-layouts: 7.08 us -> 24.3 us
    another operation x3 -> x2, other arithmetic: 9.14 us -> 0.02 us  [split3(): jnp.stack([high, middle, (rest - middle.astype(jnp.float32)).astype(jnp.b...]
    slice x1, local copies, waits for them, and re-layouts: 2.51 us -> 6.96 us  [shifted_rows(): shift_ops[kind]]
  transfers between devices with their start and end apart: 4 -> 4, of which waited for: 1 -> 1; matrix products, arithmetic and copies ran while one was open for 74% -> 29% of each run, Pallas kernels for 0% -> 25%
where the time goes in v1:
time: 154 us; the launch traced here: 153 us
  local copies, waits for them, and re-layouts  44.3 us (29%)
  Pallas kernels  38.6 us (25%)
  waiting for transfers between devices  24.7 us (16%)
  matrix products  19.3 us (13%)
  starting transfers between devices  19.1 us (12%)
  other arithmetic  6.19 us (4%)
    pallas_call x1, Pallas kernels, near_field(): pl.pallas_call(functools.partial(near_kernel, rows, group), out_shape=jax...  38.6 us
    all_to_all x1, waiting for transfers between devices, local(): lax.all_to_all(result.reshape(devices, capacity, -1), 'leaf', split_axis=...  24.7 us
    unnamed x45, local copies, waits for them, and re-layouts  24.3 us
    all_to_all x1, starting transfers between devices, local(): lax.all_to_all(jnp.concatenate([base.reshape(devices, capacity, coef_widt...  9.48 us
    gather x1, local copies, waits for them, and re-layouts, local(): base = shifted_rows(concentration[departure], departure_class, shift_ops)  9.05 us
    slice x1, local copies, waits for them, and re-layouts, shifted_rows(): shift_ops[kind]  6.96 us
    dot_general x8, matrix products, shifted_rows(): jnp.dot(gathered, shift_ops[kind], preferred_element_type=jnp.float32)  6.82 us
    all_to_all x1, starting transfers between devices, local(): lax.all_to_all(result.reshape(devices, capacity, -1), 'leaf', split_axis=...  5.78 us
  transfers between devices with their start and end apart: 4, of which 1 were waited for; matrix products, arithmetic and copies ran while one was open for 29% of the time, Pallas kernels for 25%

profile of v1, /device:TPU:0, one launch (start us, length us, event | category | flops | bytes accessed | tf_op | source)
XLA Modules:
  0.0 153.3 jit_solution(17339284319876113813)
XLA Ops:
  1.4 1.2 copy.54
  3.0 2.5 %collective-permute-start = (bf16[1024,256]{1,0:T(8,128)(2,1)S(1)}, bf16[1024,256]{1,0:T(8,128)(2,1)S(1)}, u32[]{:S(2)}, u32[]{:S(2)}) collective-permute-start(bf16[1024,256]{1,0:T(8,128)(2,1)S(1)} %pad.8.mid_ref), channel_id=1, source_target_pairs={{0,1},{1,2},{2,3},{3,4},{4,5},{5,6},{6,7},{7,8},{8,9},{9,10},{10,1... | collective-permute-start | bytes 1572872 | tf_op jit(solution)/shard_map/ppermute | solution.py:23
  5.5 1.3 collective-permute-start.1
  7.5 1.5 copy.56
  9.0 7.0 %fusion.41 = (bf16[1,220,220]{2,0,1:T(2,128)(2,1)S(1)}, bf16[1,220,220]{2,0,1:T(2,128)(2,1)}, bf16[1,220,220]{2,0,1:T(2,128)(2,1)}, bf16[1,220,220]{2,0,1:T(2,12...) fusion(bf16[8,220,220]{2,0,1:T(8,128)(2,1)} %param.26), kind=kLoop, calls=%fused_computation.87 | loop fusion | bytes 1548800 | tf_op jit(solution)/shard_map/slice | solution.py:120
  15.9 9.1 %gather_fusion = bf16[2048,220]{1,0:T(8,128)(2,1)} fusion(bf16[2048,220]{1,0:T(8,128)(2,1)S(1)} %copy.56, s32[2048]{0:T(1024)S(1)} %fusion.35), kind=kCustom, calls=%fused_computation | custom fusion | bytes 1810432 | tf_op jit(solution)/shard_map/gather | solution.py:177
  25.0 1.9 %fusion.24 = bf16[2048,220]{0,1:T(8,128)(2,1)S(1)} fusion(bf16[2048,220]{1,0:T(8,128)(2,1)} %gather_fusion, bf16[1,220,220]{2,0,1:T(2,128)(2,1)} %get-tuple-element.11), kind=kOutput, calls=%fused_computation.48 | convolution fusion | flops 198246400 | bytes 1899040 | tf_op jit(solution)/shard_map/dot_general | solution.py:120
  30.7 1.5 fusion.13
  32.2 1.5 copy.65
  34.0 1.3 pad_maximum_fusion
  35.3 9.5 %all-to-all-start = ((bf16[32,64,223]{2,1,0:T(8,128)(2,1)}), bf16[32,64,223]{2,1,0:T(8,128)(2,1)}, u32[]{:S(2)}, u32[]{:S(2)}) async-start(bf16[32,64,223]{2,1,0:T(8,128)(2,1)} %pad_maximum_fusion), calls=%async_computation | async-start | bytes 2097152 | tf_op jit(solution)/shard_map/all_to_all | solution.py:184
  45.5 12.9 %copy.55.ops_ref = bf16[27,220,660]{2,1,0:T(8,128)(2,1)} copy(bf16[27,220,660]{1,2,0:T(8,128)(2,1)} %param.17) | data formatting | bytes 15681600 | tf_op args[3]
  58.4 1.5 fusion.1
  64.6 38.6 %near_field.1 = f32[1024,660]{1,0:T(8,128)S(1)} custom-call(s32[27648]{0:T(1024)S(1)} %reshape.66.idx_ref, bf16[1024,256]{1,0:T(8,128)(2,1)S(1)} %copy-done.4, bf16[1024,256]{1,0:T(8,128)(2,1)S(1)} %copy-done.2, bf16[1024,256]{1,0:T(8,128)(2,1)S(1)} %copy-done.6, bf16[27,220,660]{2,1,0:T(8,128)(2,1)} %copy.55.ops_ref), custom_call_target="tpu_custom_call" | custom-call | flops 46714060800 | bytes 100000000 | tf_op jit(solution)/shard_map/near_field/pallas_call | solution.py:87
  103.2 1.6 %convert_reduce_fusion = f32[32,64]{1,0:T(8,128)S(1)} fusion(bf16[32,64,223]{2,1,0:T(8,128)(2,1)} %all-to-all-done), kind=kLoop, calls=%fused_computation.40 | loop fusion | flops 10240 | bytes 20480 | tf_op jit(solution)/shard_map/reduce_sum | solution.py:192
  107.3 1.1 copy-done.8
  108.5 4.5 %fusion.5 = bf16[2048,660]{0,1:T(8,128)(2,1)} fusion(bf16[1024,660]{1,0:T(8,128)(2,1)S(1)} %fusion.7, s32[1024]{0:T(1024)S(1)} %convert_add_fusion), kind=kOutput, calls=%fused_computation.8 | convolution fusion | flops 2771689472 | bytes 4059136 | tf_op jit(solution)/shard_map/dot_general | solution.py:220
  113.0 2.0 %dot_general.75 = bf16[2048,3,220]{0,2,1:T(8,128)(2,1)S(1)} reshape(bf16[2048,660]{0,1:T(8,128)(2,1)} %fusion.5) | data formatting | bytes 5406720 | tf_op jit(solution)/shard_map/dot_general | solution.py:128
  115.0 1.1 fusion.29
  116.1 2.5 %fusion.43 = f32[2048,1024]{1,0:T(8,128)S(1)} fusion(bf16[2048,220]{1,0:T(8,128)(2,1)} %bitcast.25, bf16[220,1024]{1,0:T(8,128)(2,1)S(1)} %copy-done.10), kind=kOutput, calls=%fused_computation.89 | convolution fusion | flops 922746880 | bytes 9740288 | tf_op jit(solution)/shard_map/dot_general | solution.py:126
  118.6 1.7 %fusion.18 = bf16[2048,256]{1,0:T(8,128)(2,1)} fusion(f32[2048,1024]{1,0:T(8,128)S(1)} %fusion.43, f32[2048,3,256]{2,0,1:T(8,128)S(1)} %fusion.29, f32[2048]{0:T(1024)S(1)} %convert_convert_fusion), kind=kLoop, calls=%fused_computation.26 | loop fusion | flops 4718592 | bytes 15736832 | tf_op jit(solution)/shard_map/convert_element_type | solution.py:137
  120.3 5.8 %all-to-all-start.1 = ((bf16[32,64,256]{2,1,0:T(8,128)(2,1)}), bf16[32,64,256]{2,1,0:T(8,128)(2,1)S(1)}, u32[]{:S(2)}, u32[]{:S(2)}) async-start(bf16[32,64,256]{2,1,0:T(8,128)(2,1)} %bitcast.30), calls=%async_computation.1 | async-start | bytes 2097152 | tf_op jit(solution)/shard_map/all_to_all | solution.py:229
  126.1 1.5 copy.69
  127.6 24.7 %all-to-all-done.1 = bf16[32,64,256]{2,1,0:T(8,128)(2,1)S(1)} async-done(((bf16[32,64,256]{2,1,0:T(8,128)(2,1)}), bf16[32,64,256]{2,1,0:T(8,128)(2,1)S(1)}, u32[]{:S(2)}, u32[]{:S(2)}) %all-to-all-start.1) | async-done | bytes 1048608 | tf_op jit(solution)/shard_map/all_to_all | solution.py:229
  (76 shorter events, 14.6 us)
Async XLA Ops:
  0.6 106.1 %copy-start = (bf16[8,56,220]{2,1,0:T(8,128)(2,1)S(1)}, bf16[8,56,220]{2,1,0:T(8,128)(2,1)}, u32[]{:S(2)}) copy-start(bf16[8,56,220]{2,1,0:T(8,128)(2,1)} %param.21) | copy-start | bytes 591364
  0.6 6.4 %copy-start.19 = (bf16[8,220,56]{1,2,0:T(8,128)(2,1)S(1)}, bf16[8,220,56]{1,2,0:T(8,128)(2,1)}, u32[]{:S(2)}) copy-start(bf16[8,220,56]{1,2,0:T(8,128)(2,1)} %param.18) | copy-start | bytes 591364
  3.0 13.0 %copy-start.1 = (bf16[1024,256]{1,0:T(8,128)(2,1)}, bf16[1024,256]{1,0:T(8,128)(2,1)S(1)}, u32[]{:S(2)}) copy-start(bf16[1024,256]{1,0:T(8,128)(2,1)S(1)} %pad.8.mid_ref) | copy-start | bytes 1572868
  3.0 6.0 %copy-start.17 = (s32[2048]{0:T(1024)S(1)}, s32[2048]{0:T(1024)}, u32[]{:S(2)}) copy-start(s32[2048]{0:T(1024)} %param.24) | copy-start | bytes 24580
  3.0 56.9 %collective-permute-start = (bf16[1024,256]{1,0:T(8,128)(2,1)S(1)}, bf16[1024,256]{1,0:T(8,128)(2,1)S(1)}, u32[]{:S(2)}, u32[]{:S(2)}) collective-permute-start(bf16[1024,256]{1,0:T(8,128)(2,1)S(1)} %pad.8.mid_ref), channel_id=1, source_target_pairs={{0,1},{1,2},{2,3},{3,4},{4,5},{5,6},{6,7},{7,8},{8,9},{9,10},{10,1... | collective-permute-start | bytes 1572872 | tf_op jit(solution)/shard_map/ppermute | solution.py:23
  5.5 55.2 %collective-permute-start.1 = (bf16[1024,256]{1,0:T(8,128)(2,1)S(1)}, bf16[1024,256]{1,0:T(8,128)(2,1)S(1)}, u32[]{:S(2)}, u32[]{:S(2)}) collective-permute-start(bf16[1024,256]{1,0:T(8,128)(2,1)S(1)} %pad.8.mid_ref), channel_id=1, source_target_pairs={{1,0},{2,1},{3,2},{4,3},{5,4},{6,5},{7,6},{8,7},{9,8},{10,9},{11,1... | collective-permute-start | bytes 1572872 | tf_op jit(solution)/shard_map/ppermute | solution.py:23
  25.0 1.9 %copy-start.7 = (bf16[2048,220]{1,0:T(8,128)(2,1)S(1)}, bf16[2048,220]{1,0:T(8,128)(2,1)}, u32[]{:S(2)}) copy-start(bf16[2048,220]{1,0:T(8,128)(2,1)} %gather_fusion) | copy-start | bytes 2703364
  25.0 1.9 %copy-start.12 = (bf16[1,220,220]{2,0,1:T(2,128)(2,1)S(1)}, bf16[1,220,220]{2,0,1:T(2,128)(2,1)}, u32[]{:S(2)}) copy-start(bf16[1,220,220]{2,0,1:T(2,128)(2,1)} %get-tuple-element.12) | copy-start | bytes 290404
  25.0 2.4 %copy-start.16 = (s32[2048]{0:T(1024)S(1)}, s32[2048]{0:T(1024)}, u32[]{:S(2)}) copy-start(s32[2048]{0:T(1024)} %param.25) | copy-start | bytes 24580
  25.0 2.5 %copy-start.11 = (bf16[1,220,220]{2,0,1:T(2,128)(2,1)S(1)}, bf16[1,220,220]{2,0,1:T(2,128)(2,1)}, u32[]{:S(2)}) copy-start(bf16[1,220,220]{2,0,1:T(2,128)(2,1)} %get-tuple-element.14) | copy-start | bytes 290404
  28.0 1.1 copy-start.14
  29.0 0.9 copy-start.13
  33.9 10.8 %copy-start.18 = (s32[1024,1]{0,1:T(1,128)S(1)}, s32[1024,1]{0,1:T(1,128)}, u32[]{:S(2)}) copy-start(s32[1024,1]{0,1:T(1,128)} %param.22) | copy-start | bytes 12292
  35.2 10.1 %copy-start.15 = (s32[1024,27]{0,1:T(8,128)S(1)}, s32[1024,27]{0,1:T(8,128)}, u32[]{:S(2)}) copy-start(s32[1024,27]{0,1:T(8,128)} %param.16) | copy-start | bytes 331780
  35.3 68.0 %all-to-all-start = ((bf16[32,64,223]{2,1,0:T(8,128)(2,1)}), bf16[32,64,223]{2,1,0:T(8,128)(2,1)}, u32[]{:S(2)}, u32[]{:S(2)}) async-start(bf16[32,64,223]{2,1,0:T(8,128)(2,1)} %pad_maximum_fusion), calls=%async_computation | async-start | bytes 2097152 | tf_op jit(solution)/shard_map/all_to_all | solution.py:184
  59.9 0.8 copy-start.3
  60.7 0.8 copy-start.5
  61.5 1.0 copy-start.2
  62.5 1.0 copy-start.4
  63.5 1.0 copy-start.6
  107.3 1.2 copy-start.8
  113.0 2.0 %copy-start.10 = (bf16[220,1024]{1,0:T(8,128)(2,1)S(1)}, bf16[220,1024]{1,0:T(8,128)(2,1)}, u32[]{:S(2)}) copy-start(bf16[220,1024]{1,0:T(8,128)(2,1)} %param.27) | copy-start | bytes 1351684
  120.3 5.8 %copy-start.9 = (bf16[1024,660]{1,0:T(8,128)(2,1)S(1)}, bf16[1024,660]{1,0:T(8,128)(2,1)}, u32[]{:S(2)}) copy-start(bf16[1024,660]{1,0:T(8,128)(2,1)} %copy-done.8) | copy-start | bytes 4055044
  120.3 32.0 %all-to-all-start.1 = ((bf16[32,64,256]{2,1,0:T(8,128)(2,1)}), bf16[32,64,256]{2,1,0:T(8,128)(2,1)S(1)}, u32[]{:S(2)}, u32[]{:S(2)}) async-start(bf16[32,64,256]{2,1,0:T(8,128)(2,1)} %bitcast.30), calls=%async_computation.1 | async-start | bytes 2097152 | tf_op jit(solution)/shard_map/all_to_all | solution.py:229

commit v2 on v1

v2 whole, which is shorter than its diff:
```python
import functools

import jax
import jax.numpy as jnp
from jax import lax
from jax.experimental import pallas as pl
from jax.experimental.pallas import tpu as pltpu
from jax.sharding import PartitionSpec as P

SPAN = 4


time_step = 0.5


LANES = 128


def halo(block):
    count = lax.axis_size("leaf")
    forward = [(i, i + 1) for i in range(count - 1)]
    backward = [(target, source) for source, target in forward]
    return lax.ppermute(block, "leaf", forward), lax.ppermute(block, "leaf", backward)


def lane_halves(target, at, values):
    count, width = values.shape
    target[pl.ds(at, count, stride=2), :] = values[:, :LANES]
    upper = values[:, LANES:]
    if width < 2 * LANES:
        upper = jnp.concatenate([upper, jnp.zeros((count, 2 * LANES - width), values.dtype)], axis=1)
    target[pl.ds(at + 1, count, stride=2), :] = upper


def near_kernel(rows, group, idx_ref, low_ref, mid_ref, high_ref, ops_ref, out_ref, source, picked, lhs, raw, weights, sem):
    block = pl.program_id(0)
    taps, _, depth = ops_ref.shape
    wide = 2 * LANES
    leaves = mid_ref.shape[0]
    fetch = pltpu.make_async_copy(ops_ref, raw, sem)

    def pick(turn):
        for j in range(group):
            at = (turn * group + j) * leaves + block * rows
            for r in range(rows):
                row = pl.multiple_of(idx_ref[at + r], 2)
                picked[pl.ds(2 * (j * rows + r), 2), :] = source[pl.ds(row, 2), :]

    def settle():
        for j in range(group):
            for half in range(2):
                values = picked[pl.ds(2 * j * rows + half, rows, stride=2), :]
                lhs[:, (2 * j + half) * LANES : (2 * j + half + 1) * LANES] = values.astype(jnp.bfloat16)

    def product(turn):
        at = pl.multiple_of(turn * (group * wide), group * wide)
        return lax.dot_general(
            weights[:, pl.ds(at, group * wide)],
            lhs[...],
            (((1,), (1,)), ((), ())),
            preferred_element_type=jnp.float32,
        )

    @pl.when(block == 0)
    def _():
        fetch.start()
        for part, ref in enumerate((low_ref, mid_ref, high_ref)):
            @pl.loop(0, leaves // rows)
            def _(chunk):
                values = ref[pl.ds(chunk * rows, rows), :].astype(jnp.float32)
                lane_halves(source, 2 * (part * leaves + chunk * rows), values)

    pick(0)
    settle()

    @pl.when(block == 0)
    def _():
        fetch.wait()
        for tap in range(taps):
            weights[:, tap * wide + LANES : (tap + 1) * wide] = jnp.zeros((weights.shape[0], LANES), weights.dtype)
            weights[:, tap * wide : tap * wide + depth] = raw[tap]

    out_ref[...] = jnp.zeros_like(out_ref)

    @pl.loop(0, taps // group - 1)
    def _(turn):
        out_ref[...] += product(turn)
        pick(turn + 1)
        settle()

    out_ref[...] += product(taps // group - 1)


def near_field(low, mid, high, local_rows, near_ops):
    leaves = mid.shape[0]
    taps, depth, outs = near_ops.shape
    rows = 256 if leaves % 256 == 0 else leaves
    group = 3 if taps % 3 == 0 else 1
    flat = (2 * local_rows).T.reshape(-1)
    vmem = pl.BlockSpec(memory_space=pltpu.VMEM)
    return pl.pallas_call(
        functools.partial(near_kernel, rows, group),
        out_shape=jax.ShapeDtypeStruct((outs, leaves), jnp.float32),
        grid=(leaves // rows,),
        in_specs=[
            pl.BlockSpec(memory_space=pltpu.SMEM), vmem, vmem, vmem, pl.BlockSpec(memory_space=pl.ANY)
        ],
        out_specs=pl.BlockSpec((outs, rows), lambda i: (0, i)),
        scratch_shapes=[
            pltpu.VMEM((6 * leaves, LANES), jnp.float32),
            pltpu.VMEM((2 * group * rows, LANES), jnp.float32),
            pltpu.VMEM((rows, group * 2 * LANES), jnp.bfloat16),
            pltpu.VMEM((taps, outs, depth), jnp.bfloat16),
            pltpu.VMEM((outs, taps * 2 * LANES), jnp.bfloat16),
            pltpu.SemaphoreType.DMA(()),
        ],
        compiler_params=pltpu.CompilerParams(
            dimension_semantics=("arbitrary",), vmem_limit_bytes=48 * 1024 * 1024
        ),
        cost_estimate=pl.CostEstimate(
            flops=2 * leaves * taps * 2 * LANES * outs * 5, bytes_accessed=100_000_000, transcendentals=0
        ),
        name="near_field",
    )(flat, low, mid, high, near_ops.transpose(0, 2, 1))


def base_kernel(rows, capacity, idx_ref, field_ref, class_ref, ops_ref, carried_ref, out_ref, source, picked, lhs, weights):
    block = pl.program_id(0)
    kinds, depth, outs = ops_ref.shape
    wide = 2 * LANES

    @pl.when(block == 0)
    def _():
        @pl.loop(0, field_ref.shape[0] // rows)
        def _(chunk):
            values = field_ref[pl.ds(chunk * rows, rows), :].astype(jnp.float32)
            lane_halves(source, 2 * chunk * rows, values)

        for kind in range(kinds):
            weights[kind * wide : (kind + 1) * wide, LANES:] = jnp.zeros((wide, LANES), weights.dtype)
            weights[kind * wide : (kind + 1) * wide, :outs] = jnp.concatenate(
                [ops_ref[kind], jnp.zeros((wide - depth, outs), ops_ref.dtype)], axis=0
            )

    for r in range(rows):
        row = pl.multiple_of(2 * idx_ref[block * rows + r], 2)
        picked[2 * r : 2 * r + 2, :] = source[pl.ds(row, 2), :]
    halves = [picked[pl.ds(half, rows, stride=2), :] for half in range(2)]
    for kind in range(kinds):
        chosen = class_ref[...] == kind
        for half in range(2):
            at = kind * wide + half * LANES
            lhs[:, at : at + LANES] = jnp.where(chosen, halves[half], 0.0).astype(jnp.bfloat16)
    total = jnp.dot(lhs[...], weights[...], preferred_element_type=jnp.float32)
    extra = carried_ref[...].astype(jnp.float32)
    out_ref[...] = (total + jnp.concatenate([extra] * (rows // capacity), axis=0)).astype(jnp.bfloat16)


def base_rows(concentration, departure, departure_class, shift_ops, carried):
    slots, width = concentration.shape
    capacity = carried.shape[0]
    kinds = shift_ops.shape[0]
    rows = 256 if slots % 256 == 0 and 256 % capacity == 0 else slots
    wide = 2 * LANES
    vmem = pl.BlockSpec(memory_space=pltpu.VMEM)
    return pl.pallas_call(
        functools.partial(base_kernel, rows, capacity),
        out_shape=jax.ShapeDtypeStruct((slots, wide), jnp.bfloat16),
        grid=(slots // rows,),
        in_specs=[
            pl.BlockSpec(memory_space=pltpu.SMEM),
            vmem,
            pl.BlockSpec((rows, 1), lambda i: (i, 0)),
            vmem,
            vmem,
        ],
        out_specs=pl.BlockSpec((rows, wide), lambda i: (i, 0)),
        scratch_shapes=[
            pltpu.VMEM((2 * slots, LANES), jnp.float32),
            pltpu.VMEM((2 * rows, LANES), jnp.float32),
            pltpu.VMEM((rows, kinds * wide), jnp.bfloat16),
            pltpu.VMEM((kinds * wide, wide), jnp.bfloat16),
        ],
        compiler_params=pltpu.CompilerParams(
            dimension_semantics=("arbitrary",), vmem_limit_bytes=32 * 1024 * 1024
        ),
        cost_estimate=pl.CostEstimate(
            flops=2 * slots * kinds * wide * wide, bytes_accessed=4 * slots * wide, transcendentals=0
        ),
        name="base_rows",
    )(departure, concentration, departure_class[:, None], shift_ops, carried)


MESH = pl.DeviceIdType.MESH


def return_kernel(
    n, group, slot_ref, alive_ref, near_ref, far_ref, got_ref, eval_ref, vel_ref, adv_ref,
    moved, spread, spread_low, values_op, result, send_sem, recv_sem,
):
    me = lax.axis_index("leaf")
    capacity, wide = got_ref.shape[1], got_ref.shape[2]
    depth, nodes = eval_ref.shape[0], eval_ref.shape[1] // 4
    outs, leaves = near_ref.shape
    padded = moved.shape[0]
    rows = group * capacity
    barrier = pltpu.get_barrier_semaphore()

    @pl.loop(1, n)
    def _(turn):
        pl.semaphore_signal(barrier, inc=1, device_id=(lax.rem(me + turn, n),), device_id_type=MESH)

    far = far_ref[...]
    for at in range(0, leaves, LANES):
        block = ((near_ref[:, at : at + LANES] + far) * alive_ref[:, at : at + LANES]).astype(jnp.bfloat16)
        vel_ref[:, at : at + LANES] = block
        moved[:, at : at + LANES] = jnp.concatenate(
            [block, jnp.ones((padded - outs, LANES), jnp.bfloat16)], axis=0
        )
    spread[...] = jnp.zeros_like(spread)
    for j in range(3):
        spread[j * depth : (j + 1) * depth, j * nodes : (j + 1) * nodes] = eval_ref[:, :nodes].astype(jnp.float32)
    spread_low[...] = spread[...].astype(jnp.bfloat16)
    values_op[...] = jnp.concatenate(
        [eval_ref[...], jnp.zeros((wide - depth, 4 * nodes), jnp.bfloat16)], axis=0
    )
    pl.semaphore_wait(barrier, n - 1)

    def copy(turn, landing):
        return pltpu.make_async_remote_copy(
            src_ref=result.at[turn],
            dst_ref=adv_ref.at[landing],
            send_sem=send_sem.at[turn],
            recv_sem=recv_sem.at[turn],
            device_id=(lax.rem(me + turn, n),),
            device_id_type=MESH,
        )

    @pl.loop(0, n // group)
    def _(step):
        ids = lax.broadcasted_iota(jnp.int32, (rows, 1), 0) + step * rows
        placed = jnp.where(slot_ref[...] == ids, 1.0, 0.0).astype(jnp.bfloat16)
        sent = lax.dot_general(
            placed, moved[...], (((1,), (1,)), ((), ())), preferred_element_type=jnp.float32
        )
        speeds = jnp.dot(sent.astype(jnp.bfloat16), spread_low[...], preferred_element_type=jnp.float32)
        base = jnp.concatenate(
            [got_ref[lax.rem(me + step * group + j, n)] for j in range(group)], axis=0
        )
        values = jnp.dot(base, values_op[...], preferred_element_type=jnp.float32)
        correction = speeds[:, :nodes] * values[:, nodes : 2 * nodes]
        correction = correction + speeds[:, nodes : 2 * nodes] * values[:, 2 * nodes : 3 * nodes]
        correction = correction + speeds[:, 2 * nodes :] * values[:, 3 * nodes :]
        filled = sent[:, outs : outs + 1]
        final = (filled * (values[:, :nodes] - time_step * correction)).astype(jnp.bfloat16)
        for j in range(group):
            result[step * group + j] = final[j * capacity : (j + 1) * capacity]
        for j in range(group):
            if j:
                copy(step * group + j, me).start()
            else:
                @pl.when(step > 0)
                def _():
                    copy(step * group, me).start()

    adv_ref[me] = result[0]

    @pl.loop(1, n)
    def _(turn):
        copy(turn, lax.rem(me - turn + n, n)).wait()


def advect_return(slot, alive, near, far, got, eval_ops):
    n, capacity, wide = got.shape
    depth, columns = eval_ops.shape
    outs, leaves = near.shape
    nodes = columns // 4
    group = 256 // capacity if 256 % capacity == 0 and n % (256 // capacity) == 0 else 1
    padded = -(-(outs + 1) // (2 * LANES)) * (2 * LANES)
    vmem = pl.BlockSpec(memory_space=pltpu.VMEM)
    return pl.pallas_call(
        functools.partial(return_kernel, n, group),
        out_shape=(
            jax.ShapeDtypeStruct((outs, leaves), jnp.bfloat16),
            jax.ShapeDtypeStruct((n, capacity, nodes), jnp.bfloat16),
        ),
        in_specs=[vmem] * 6,
        out_specs=(vmem, vmem),
        scratch_shapes=[
            pltpu.VMEM((padded, leaves), jnp.bfloat16),
            pltpu.VMEM((padded, 3 * nodes), jnp.float32),
            pltpu.VMEM((padded, 3 * nodes), jnp.bfloat16),
            pltpu.VMEM((wide, columns), jnp.bfloat16),
            pltpu.VMEM((n, capacity, nodes), jnp.bfloat16),
            pltpu.SemaphoreType.DMA((n,)),
            pltpu.SemaphoreType.DMA((n,)),
        ],
        compiler_params=pltpu.CompilerParams(
            collective_id=0, has_side_effects=True, vmem_limit_bytes=48 * 1024 * 1024
        ),
        cost_estimate=pl.CostEstimate(
            flops=2 * n * capacity * (leaves * padded + padded * 3 * nodes + wide * columns),
            bytes_accessed=10_000_000,
            transcendentals=0,
        ),
        name="advect_return",
    )(slot, alive, near, far, got, eval_ops)


def rounded(values):
    return lax.reduce_precision(values, exponent_bits=8, mantissa_bits=7)


def split3(values):
    high = rounded(values)
    middle = rounded(values - high)
    low = rounded(values - high - middle)
    return jnp.stack([high, middle, low], axis=-1).astype(jnp.bfloat16)


def local(
    density,
    vel_mask,
    near_list,
    near_ops,
    upward_ops,
    coupling_operators,
    coarse_weights,
    downward_ops,
    conc_owner,
    concentration,
    departure,
    departure_class,
    shift_ops,
    eval_ops,
):
    leaves = density.shape[0]
    coef_width = density.shape[1]
    devices = lax.axis_size("leaf")
    my_index = lax.axis_index("leaf")
    alive = vel_mask.astype(jnp.float32)
    live_density = (density.astype(jnp.float32) * alive[:, None]).astype(jnp.bfloat16)
    wide = jnp.pad(live_density, ((0, 0), (0, 2 * LANES - coef_width)))
    low, high = halo(wide)
    local_rows = near_list - my_index * leaves + leaves
    nearby_field = near_field(low, wide, high, local_rows, near_ops)
    parts = jnp.einsum(
        "gop,opq->goq",
        live_density.reshape(-1, 8, coef_width),
        upward_ops,
        preferred_element_type=jnp.float32,
    )
    own_part = jnp.sum(parts, axis=(0, 1))
    slots_here = concentration.shape[0]
    capacity = slots_here // devices
    densities = own_part.shape[0]
    columns = -(-densities // capacity)
    carried = split3(jnp.pad(own_part, (0, columns * capacity - densities)))
    carried = jnp.pad(
        carried.reshape(capacity, 3 * columns),
        ((0, 0), (coef_width, 2 * LANES - coef_width - 3 * columns)),
    )
    base = base_rows(concentration, departure, departure_class, shift_ops, carried)
    got = lax.all_to_all(
        base.reshape(devices, capacity, -1), "leaf", split_axis=0, concat_axis=0, tiled=True
    )
    all_parts = jnp.sum(
        got[:, :, coef_width : coef_width + 3 * columns]
        .astype(jnp.float32)
        .reshape(devices, columns * capacity, 3),
        axis=2,
    )[:, :densities]
    moments = jnp.sum(all_parts.reshape(devices // SPAN, SPAN, densities), axis=1)
    my_box = my_index // SPAN
    expanded = jnp.dot(moments, coupling_operators, precision=lax.Precision.HIGHEST)
    weight_row = lax.dynamic_slice_in_dim(coarse_weights, my_box, 1, 0)
    own_expansion = jnp.dot(weight_row, expanded, precision=lax.Precision.HIGHEST)
    box_far = jnp.einsum(
        "jq,oqp->jpo",
        own_expansion.reshape(3, -1),
        downward_ops.astype(jnp.float32),
        precision=lax.Precision.HIGHEST,
    )
    far = jnp.tile(box_far.reshape(3 * coef_width, 8), (1, LANES // 8))
    owner = conc_owner[:, 0]
    onehot = owner[:, None] == jnp.arange(devices, dtype=jnp.int32)[None, :]
    order = jnp.arange(leaves, dtype=jnp.int32)
    earlier = (order[None, :] < order[:, None]).astype(jnp.bfloat16)
    before = jnp.dot(earlier, onehot.astype(jnp.bfloat16), preferred_element_type=jnp.float32)
    rank = jnp.sum(jnp.where(onehot, before, 0.0), axis=1).astype(jnp.int32)
    relative = lax.rem(owner - my_index + devices, devices)
    send_slot = jnp.where(vel_mask > 0, relative * capacity + rank, -1)
    velocity, advected = advect_return(
        send_slot[None, :], alive[None, :], nearby_field, far, got, eval_ops
    )
    return (velocity.T, advected.reshape(slots_here, -1))


def solution(mesh):
    placed = (
        P("leaf", None),
        P("leaf"),
        P("leaf", None),
        P(),
        P(),
        P(),
        P(),
        P(),
        P("leaf", None),
        P("leaf", None),
        P("leaf"),
        P("leaf"),
        P(),
        P(),
    )
    return jax.shard_map(
        local,
        mesh=mesh,
        in_specs=placed,
        out_specs=(P("leaf", None), P("leaf", None)),
        check_vma=False,
    )
```

time: 154 us -> 114 us (0.74)
  the two profiles are of different devices: /device:TPU:0 before, /device:TPU:15 now
where the time goes in v2:
time: 114 us; the launch traced here: 113 us
  Pallas kernels  87.1 us (76%)
  starting transfers between devices  11.9 us (10%)
  local copies, waits for them, and re-layouts  7.75 us (7%)
  matrix products  3.86 us (3%)
  other arithmetic  1.76 us (2%)
    pallas_call x1, Pallas kernels, near_field(): pl.pallas_call(functools.partial(near_kernel, rows, group), out_shape=jax...  44.4 us
    pallas_call x1, Pallas kernels, advect_return(): pl.pallas_call(functools.partial(return_kernel, n, group), out_shape=(jax...  34.2 us
    pallas_call x1, Pallas kernels, base_rows(): pl.pallas_call(functools.partial(base_kernel, rows, capacity), out_shape=...  8.41 us
    unnamed x21, local copies, waits for them, and re-layouts  6.71 us
    all_to_all x1, starting transfers between devices, local(): lax.all_to_all(base.reshape(devices, capacity, -1), 'leaf', split_axis=0,...  6.26 us
    ppermute x1, starting transfers between devices, halo(): lax.ppermute(block, 'leaf', forward)  3.67 us
  transfers between devices with their start and end apart: 3, of which 0 were waited for; matrix products, arithmetic and copies ran while one was open for 4% of the time, Pallas kernels for 47%

profile of v2, /device:TPU:15, one launch (start us, length us, event | category | flops | bytes accessed | tf_op | source)
XLA Modules:
  0.0 113.2 jit_solution(15759466367082301339)
XLA Ops:
  0.7 1.3 %fusion.2 = f32[1024]{0:T(1024)S(1)} fusion(s32[1024]{0:T(1024)} %bitcast.53), kind=kOutput, calls=%fused_computation.3 | convolution fusion | flops 68287488 | bytes 8192 | tf_op jit(solution)/shard_map/dot_general | solution.py:389
  2.0 1.2 %copy.47 = bf16[1024,220]{1,0:T(8,128)(2,1)S(1)} copy(bf16[1024,220]{0,1:T(8,128)(2,1)} %param.14) | data formatting | bytes 901120 | tf_op args[0]
  3.2 0.8 fusion.22
  4.0 0.2 multiply_convert_fusion
  4.3 3.7 %collective-permute-start = (bf16[1024,256]{1,0:T(8,128)(2,1)S(1)}, bf16[1024,256]{1,0:T(8,128)(2,1)S(1)}, u32[]{:S(2)}, u32[]{:S(2)}) collective-permute-start(bf16[1024,256]{1,0:T(8,128)(2,1)S(1)} %pad.12.mid_ref), channel_id=1, source_target_pairs={{0,1},{1,2},{2,3},{3,4},{4,5},{5,6},{6,7},{7,8},{8,9},{9,10},{10,1... | collective-permute-start | bytes 1572872 | tf_op jit(solution)/shard_map/ppermute | solution.py:23
  8.0 1.9 %collective-permute-start.1 = (bf16[1024,256]{1,0:T(8,128)(2,1)S(1)}, bf16[1024,256]{1,0:T(8,128)(2,1)}, u32[]{:S(2)}, u32[]{:S(2)}) collective-permute-start(bf16[1024,256]{1,0:T(8,128)(2,1)S(1)} %pad.12.mid_ref), channel_id=1, source_target_pairs={{1,0},{2,1},{3,2},{4,3},{5,4},{6,5},{7,6},{8,7},{9,8},{10,9},{11,1... | collective-permute-start | bytes 1572872 | tf_op jit(solution)/shard_map/ppermute | solution.py:23
  9.9 0.2 fusion.27
  10.2 1.3 %fusion.3 = f32[56]{0:T(128)S(1)} fusion(bf16[8,220,56]{1,2,0:T(8,128)(2,1)} %param.18, bf16[128,8,220]{2,1,0:T(8,128)(2,1)S(1)} %fusion.27), kind=kOutput, calls=%fused_computation.6 | convolution fusion | flops 25238472 | bytes 647904 | tf_op jit(solution)/shard_map/gop,opq->goq/dot_general | solution.py:347
  11.5 0.1 copy.49
  11.7 0.5 copy.50.field_ref
  12.3 0.4 copy.51.class_ref
  12.6 1.4 %copy.52.ops_ref = bf16[8,220,220]{2,1,0:T(8,128)(2,1)S(1)} copy(bf16[8,220,220]{2,0,1:T(8,128)(2,1)} %param.26) | data formatting | bytes 1548800 | tf_op args[12]
  14.0 8.4 %base_rows.1 = bf16[2048,256]{1,0:T(8,128)(2,1)} custom-call(s32[2048]{0:T(1024)S(1)} %copy-done.2, bf16[2048,220]{1,0:T(8,128)(2,1)S(1)} %copy.50.field_ref, s32[2048,1]{1,0:T(8,128)S(1)} %copy.51.class_ref, bf16[8,220,220]{2,1,0:T(8,128)(2,1)S(1)} %copy.52.ops_ref, bf16[64,256]{1,0:T(8,128)(2,1)S(1)} %pad.14.carried_ref), custom_call_target="tpu_custom_call" | custom-call | flops 2147483648 | bytes 2097152 | tf_op jit(solution)/shard_map/base_rows/pallas_call | solution.py:166
  22.4 6.3 %all-to-all-start = ((bf16[32,64,256]{2,1,0:T(8,128)(2,1)}), bf16[32,64,256]{2,1,0:T(8,128)(2,1)S(1)}, u32[]{:S(2)}, u32[]{:S(2)}) async-start(bf16[32,64,256]{2,1,0:T(8,128)(2,1)} %bitcast.13), calls=%async_computation | async-start | bytes 2097152 | tf_op jit(solution)/shard_map/all_to_all | solution.py:364
  28.8 44.4 %near_field.1.near_ref = f32[660,1024]{1,0:T(8,128)S(1)} custom-call(s32[27648]{0:T(1024)S(1)} %reshape.31.idx_ref, bf16[1024,256]{1,0:T(8,128)(2,1)S(1)} %collective-permute-done.low_ref, bf16[1024,256]{1,0:T(8,128)(2,1)S(1)} %pad.12.mid_ref, bf16[1024,256]{1,0:T(8,128)(2,1)} %collective-permute-done.1.high_ref, bf16[27,660,220]{2,1,0:T(8,128)(2,1)} %bitcast.55), custom_call_target="tpu_custom_call" | custom-call | flops 46714060800 | bytes 100000000 | tf_op jit(solution)/shard_map/near_field/pallas_call | solution.py:101
  73.3 1.5 %copy-done.3 = f32[660,1024]{1,0:T(8,128)} copy-done((f32[660,1024]{1,0:T(8,128)}, f32[660,1024]{1,0:T(8,128)S(1)}, u32[]{:S(2)}) %copy-start.3) | copy-done | bytes 2703384
  74.8 0.5 convert_reduce_fusion
  75.4 0.1 convolution_bitcast_fusion.2
  75.6 0.8 fusion.6
  76.4 0.2 convolution_bitcast_fusion
  76.8 0.2 copy.54.far_ref
  77.0 34.2 %advect_return.1 = (bf16[660,1024]{1,0:T(8,128)(2,1)S(1)}, bf16[32,64,256]{2,1,0:T(8,128)(2,1)S(1)}) custom-call(s32[1,1024]{1,0:T(1,128)S(1)} %bitcast.50, f32[1,1024]{1,0:T(1,128)S(1)} %bitcast.49, f32[660,1024]{1,0:T(8,128)} %copy-done.3, f32[660,128]{1,0:T(8,128)S(1)} %copy.54.far_ref, bf16[32,64,256]{2,1,0:T(8,128)(2,1)S(1)} %all-to-all-done.got_ref, ...), custom_call_target="tpu_custom_call" | custom-call | flops 6710886400 | bytes 10000000 | tf_op jit(solution)/shard_map/advect_return/pallas_call | solution.py:281
  111.2 1.1 copy.68
  112.3 1.0 copy.69
  (28 shorter events, 0.5 us)
Async XLA Ops:
  0.6 75.8 %copy-start = (bf16[8,56,220]{2,1,0:T(8,128)(2,1)S(1)}, bf16[8,56,220]{2,1,0:T(8,128)(2,1)}, u32[]{:S(2)}) copy-start(bf16[8,56,220]{2,1,0:T(8,128)(2,1)} %param.21) | copy-start | bytes 591364
  0.6 11.1 %copy-start.4 = (bf16[2048,220]{0,1:T(8,128)(2,1)S(1)}, bf16[2048,220]{0,1:T(8,128)(2,1)}, u32[]{:S(2)}) copy-start(bf16[2048,220]{0,1:T(8,128)(2,1)} %param.23) | copy-start | bytes 2703364
  0.7 11.6 %copy-start.7 = (s32[2048]{0:T(1024)S(1)}, s32[2048]{0:T(1024)}, u32[]{:S(2)}) copy-start(s32[2048]{0:T(1024)} %param.25) | copy-start | bytes 24580
  4.0 10.0 %copy-start.2 = (s32[2048]{0:T(1024)S(1)}, s32[2048]{0:T(1024)}, u32[]{:S(2)}) copy-start(s32[2048]{0:T(1024)} %idx_ref.1) | copy-start | bytes 24580
  4.3 24.5 %collective-permute-start = (bf16[1024,256]{1,0:T(8,128)(2,1)S(1)}, bf16[1024,256]{1,0:T(8,128)(2,1)S(1)}, u32[]{:S(2)}, u32[]{:S(2)}) collective-permute-start(bf16[1024,256]{1,0:T(8,128)(2,1)S(1)} %pad.12.mid_ref), channel_id=1, source_target_pairs={{0,1},{1,2},{2,3},{3,4},{4,5},{5,6},{6,7},{7,8},{8,9},{9,10},{10,1... | collective-permute-start | bytes 1572872 | tf_op jit(solution)/shard_map/ppermute | solution.py:23
  8.0 20.8 %collective-permute-start.1 = (bf16[1024,256]{1,0:T(8,128)(2,1)S(1)}, bf16[1024,256]{1,0:T(8,128)(2,1)}, u32[]{:S(2)}, u32[]{:S(2)}) collective-permute-start(bf16[1024,256]{1,0:T(8,128)(2,1)S(1)} %pad.12.mid_ref), channel_id=1, source_target_pairs={{1,0},{2,1},{3,2},{4,3},{5,4},{6,5},{7,6},{8,7},{9,8},{10,9},{11,1... | collective-permute-start | bytes 1572872 | tf_op jit(solution)/shard_map/ppermute | solution.py:23
  14.0 14.7 %copy-start.5 = (s32[1024,27]{0,1:T(8,128)S(1)}, s32[1024,27]{0,1:T(8,128)}, u32[]{:S(2)}) copy-start(s32[1024,27]{0,1:T(8,128)} %param.16) | copy-start | bytes 331780
  22.4 52.4 %all-to-all-start = ((bf16[32,64,256]{2,1,0:T(8,128)(2,1)}), bf16[32,64,256]{2,1,0:T(8,128)(2,1)S(1)}, u32[]{:S(2)}, u32[]{:S(2)}) async-start(bf16[32,64,256]{2,1,0:T(8,128)(2,1)} %bitcast.13), calls=%async_computation | async-start | bytes 2097152 | tf_op jit(solution)/shard_map/all_to_all | solution.py:364
  28.8 46.6 %copy-start.6 = (f32[56,168]{1,0:T(8,128)S(1)}, f32[56,168]{1,0:T(8,128)}, u32[]{:S(2)}) copy-start(f32[56,168]{1,0:T(8,128)} %param.19) | copy-start | bytes 112900
  28.8 48.1 %copy-start.1 = (bf16[220,1024]{1,0:T(8,128)(2,1)S(1)}, bf16[220,1024]{1,0:T(8,128)(2,1)}, u32[]{:S(2)}) copy-start(bf16[220,1024]{1,0:T(8,128)(2,1)} %eval_ref.1) | copy-start | bytes 1351684
  73.3 1.5 %copy-start.3 = (f32[660,1024]{1,0:T(8,128)}, f32[660,1024]{1,0:T(8,128)S(1)}, u32[]{:S(2)}) copy-start(f32[660,1024]{1,0:T(8,128)S(1)} %near_field.1.near_ref) | copy-start | bytes 8110084

commit v3 on v2

--- a/solution.py
+++ b/solution.py
@@ -16,15 +16,12 @@
 LANES = 128
 
 
-def halo(block):
-    count = lax.axis_size("leaf")
-    forward = [(i, i + 1) for i in range(count - 1)]
-    backward = [(target, source) for source, target in forward]
-    return lax.ppermute(block, "leaf", forward), lax.ppermute(block, "leaf", backward)
+MESH = pl.DeviceIdType.MESH
 
 
 def lane_halves(target, at, values):
     count, width = values.shape
+    target = target.reshape(2 * target.shape[0], LANES)
     target[pl.ds(at, count, stride=2), :] = values[:, :LANES]
     upper = values[:, LANES:]
     if width < 2 * LANES:
@@ -32,24 +29,23 @@
     target[pl.ds(at + 1, count, stride=2), :] = upper
 
 
-def near_kernel(rows, group, idx_ref, low_ref, mid_ref, high_ref, ops_ref, out_ref, source, picked, lhs, raw, weights, sem):
+def near_kernel(rows, group, idx_ref, low_ref, mid_ref, high_ref, ops_ref, out_ref, source, picked, lhs, weights):
     block = pl.program_id(0)
     taps, _, depth = ops_ref.shape
     wide = 2 * LANES
     leaves = mid_ref.shape[0]
-    fetch = pltpu.make_async_copy(ops_ref, raw, sem)
 
     def pick(turn):
         for j in range(group):
             at = (turn * group + j) * leaves + block * rows
             for r in range(rows):
-                row = pl.multiple_of(idx_ref[at + r], 2)
-                picked[pl.ds(2 * (j * rows + r), 2), :] = source[pl.ds(row, 2), :]
+                picked[j * rows + r] = source[idx_ref[at + r]]
 
     def settle():
+        flat = picked.reshape(2 * group * rows, LANES)
         for j in range(group):
             for half in range(2):
-                values = picked[pl.ds(2 * j * rows + half, rows, stride=2), :]
+                values = flat[pl.ds(2 * j * rows + half, rows, stride=2), :]
                 lhs[:, (2 * j + half) * LANES : (2 * j + half + 1) * LANES] = values.astype(jnp.bfloat16)
 
     def product(turn):
@@ -63,7 +59,6 @@
 
     @pl.when(block == 0)
     def _():
-        fetch.start()
         for part, ref in enumerate((low_ref, mid_ref, high_ref)):
             @pl.loop(0, leaves // rows)
             def _(chunk):
@@ -75,10 +70,9 @@
 
     @pl.when(block == 0)
     def _():
-        fetch.wait()
         for tap in range(taps):
             weights[:, tap * wide + LANES : (tap + 1) * wide] = jnp.zeros((weights.shape[0], LANES), weights.dtype)
-            weights[:, tap * wide : tap * wide + depth] = raw[tap]
+            weights[:, tap * wide : tap * wide + depth] = ops_ref[tap]
 
     out_ref[...] = jnp.zeros_like(out_ref)
 
@@ -96,26 +90,22 @@
     taps, depth, outs = near_ops.shape
     rows = 256 if leaves % 256 == 0 else leaves
     group = 3 if taps % 3 == 0 else 1
-    flat = (2 * local_rows).T.reshape(-1)
+    flat = local_rows.T.reshape(-1)
     vmem = pl.BlockSpec(memory_space=pltpu.VMEM)
     return pl.pallas_call(
         functools.partial(near_kernel, rows, group),
         out_shape=jax.ShapeDtypeStruct((outs, leaves), jnp.float32),
         grid=(leaves // rows,),
-        in_specs=[
-            pl.BlockSpec(memory_space=pltpu.SMEM), vmem, vmem, vmem, pl.BlockSpec(memory_space=pl.ANY)
-        ],
+        in_specs=[pl.BlockSpec(memory_space=pltpu.SMEM), vmem, vmem, vmem, vmem],
         out_specs=pl.BlockSpec((outs, rows), lambda i: (0, i)),
         scratch_shapes=[
-            pltpu.VMEM((6 * leaves, LANES), jnp.float32),
-            pltpu.VMEM((2 * group * rows, LANES), jnp.float32),
+            pltpu.VMEM((3 * leaves, 2, LANES), jnp.float32),
+            pltpu.VMEM((group * rows, 2, LANES), jnp.float32),
             pltpu.VMEM((rows, group * 2 * LANES), jnp.bfloat16),
-            pltpu.VMEM((taps, outs, depth), jnp.bfloat16),
             pltpu.VMEM((outs, taps * 2 * LANES), jnp.bfloat16),
-            pltpu.SemaphoreType.DMA(()),
         ],
         compiler_params=pltpu.CompilerParams(
-            dimension_semantics=("arbitrary",), vmem_limit_bytes=48 * 1024 * 1024
+            dimension_semantics=("arbitrary",), vmem_limit_bytes=36 * 1024 * 1024
         ),
         cost_estimate=pl.CostEstimate(
             flops=2 * leaves * taps * 2 * LANES * outs * 5, bytes_accessed=100_000_000, transcendentals=0
@@ -124,74 +114,108 @@
     )(flat, low, mid, high, near_ops.transpose(0, 2, 1))
 
 
-def base_kernel(rows, capacity, idx_ref, field_ref, class_ref, ops_ref, carried_ref, out_ref, source, picked, lhs, weights):
-    block = pl.program_id(0)
+def base_kernel(
+    rows, n, idx_ref, field_ref, class_ref, ops_ref, carried_ref, wide_ref, out_ref, low_ref, high_ref,
+    source, picked, lhs, weights, send_sem, recv_sem,
+):
+    me = lax.axis_index("leaf")
+    right, left = lax.rem(me + 1, n), lax.rem(me + n - 1, n)
     kinds, depth, outs = ops_ref.shape
     wide = 2 * LANES
-
-    @pl.when(block == 0)
-    def _():
-        @pl.loop(0, field_ref.shape[0] // rows)
-        def _(chunk):
-            values = field_ref[pl.ds(chunk * rows, rows), :].astype(jnp.float32)
-            lane_halves(source, 2 * chunk * rows, values)
-
+    slots = field_ref.shape[0]
+    capacity = carried_ref.shape[0]
+    barrier = pltpu.get_barrier_semaphore()
+    for neighbour in (left, right):
+        pl.semaphore_signal(barrier, inc=1, device_id=(neighbour,), device_id_type=MESH)
+
+    @pl.loop(0, slots // rows)
+    def _(chunk):
+        values = field_ref[pl.ds(chunk * rows, rows), :].astype(jnp.float32)
+        lane_halves(source, 2 * chunk * rows, values)
+
+    pl.semaphore_wait(barrier, 2)
+    copies = [
+        pltpu.make_async_remote_copy(
+            src_ref=wide_ref,
+            dst_ref=landing,
+            send_sem=send_sem.at[which],
+            recv_sem=recv_sem.at[which],
+            device_id=(neighbour,),
+            device_id_type=MESH,
+        )
+        for which, (landing, neighbour) in enumerate(((low_ref, right), (high_ref, left)))
+    ]
+    for copy in copies:
+        copy.start()
+
+    for kind in range(kinds):
+        weights[kind * wide : (kind + 1) * wide, LANES:] = jnp.zeros((wide, LANES), weights.dtype)
+        weights[kind * wide : (kind + 1) * wide, :outs] = jnp.concatenate(
+            [ops_ref[kind], jnp.zeros((wide - depth, outs), ops_ref.dtype)], axis=0
+        )
+    extra = jnp.concatenate([carried_ref[...].astype(jnp.float32)] * (rows // capacity), axis=0)
+
+    @pl.loop(0, slots // rows)
+    def _(block):
+        for r in range(rows):
+            picked[r] = source[idx_ref[block * rows + r]]
+        flat = picked.reshape(2 * rows, LANES)
+        halves = [flat[pl.ds(half, rows, stride=2), :] for half in range(2)]
+        here = pl.ds(pl.multiple_of(block * rows, rows), rows)
+        classes = class_ref[here, :]
         for kind in range(kinds):
-            weights[kind * wide : (kind + 1) * wide, LANES:] = jnp.zeros((wide, LANES), weights.dtype)
-            weights[kind * wide : (kind + 1) * wide, :outs] = jnp.concatenate(
-                [ops_ref[kind], jnp.zeros((wide - depth, outs), ops_ref.dtype)], axis=0
-            )
-
-    for r in range(rows):
-        row = pl.multiple_of(2 * idx_ref[block * rows + r], 2)
-        picked[2 * r : 2 * r + 2, :] = source[pl.ds(row, 2), :]
-    halves = [picked[pl.ds(half, rows, stride=2), :] for half in range(2)]
-    for kind in range(kinds):
-        chosen = class_ref[...] == kind
-        for half in range(2):
-            at = kind * wide + half * LANES
-            lhs[:, at : at + LANES] = jnp.where(chosen, halves[half], 0.0).astype(jnp.bfloat16)
-    total = jnp.dot(lhs[...], weights[...], preferred_element_type=jnp.float32)
-    extra = carried_ref[...].astype(jnp.float32)
-    out_ref[...] = (total + jnp.concatenate([extra] * (rows // capacity), axis=0)).astype(jnp.bfloat16)
-
-
-def base_rows(concentration, departure, departure_class, shift_ops, carried):
-    slots, width = concentration.shape
+            for half in range(2):
+                at = kind * wide + half * LANES
+                lhs[:, at : at + LANES] = jnp.where(classes == kind, halves[half], 0.0).astype(jnp.bfloat16)
+        total = jnp.dot(lhs[...], weights[...], preferred_element_type=jnp.float32)
+        out_ref[here, :] = (total + extra).astype(jnp.bfloat16)
+
+    for copy in copies:
+        copy.wait()
+
+
+def base_rows(concentration, departure, departure_class, shift_ops, carried, own):
+    slots, _ = concentration.shape
     capacity = carried.shape[0]
     kinds = shift_ops.shape[0]
     rows = 256 if slots % 256 == 0 and 256 % capacity == 0 else slots
     wide = 2 * LANES
     vmem = pl.BlockSpec(memory_space=pltpu.VMEM)
     return pl.pallas_call(
-        functools.partial(base_kernel, rows, capacity),
-        out_shape=jax.ShapeDtypeStruct((slots, wide), jnp.bfloat16),
-        grid=(slots // rows,),
-        in_specs=[
-            pl.BlockSpec(memory_space=pltpu.SMEM),
-            vmem,
-            pl.BlockSpec((rows, 1), lambda i: (i, 0)),
-            vmem,
-            vmem,
-        ],
-        out_specs=pl.BlockSpec((rows, wide), lambda i: (i, 0)),
+        functools.partial(base_kernel, rows, slots // capacity),
+        out_shape=(
+            jax.ShapeDtypeStruct((slots, wide), jnp.bfloat16),
+            jax.ShapeDtypeStruct(own.shape, jnp.bfloat16),
+            jax.ShapeDtypeStruct(own.shape, jnp.bfloat16),
+        ),
+        in_specs=[pl.BlockSpec(memory_space=pltpu.SMEM)] + [vmem] * 5,
+        out_specs=(vmem, vmem, vmem),
         scratch_shapes=[
-            pltpu.VMEM((2 * slots, LANES), jnp.float32),
-            pltpu.VMEM((2 * rows, LANES), jnp.float32),
+            pltpu.VMEM((slots, 2, LANES), jnp.float32),
+            pltpu.VMEM((rows, 2, LANES), jnp.float32),
             pltpu.VMEM((rows, kinds * wide), jnp.bfloat16),
             pltpu.VMEM((kinds * wide, wide), jnp.bfloat16),
+            pltpu.SemaphoreType.DMA((2,)),
+            pltpu.SemaphoreType.DMA((2,)),
         ],
         compiler_params=pltpu.CompilerParams(
-            dimension_semantics=("arbitrary",), vmem_limit_bytes=32 * 1024 * 1024
+            collective_id=1, has_side_effects=True, vmem_limit_bytes=24 * 1024 * 1024
         ),
         cost_estimate=pl.CostEstimate(
             flops=2 * slots * kinds * wide * wide, bytes_accessed=4 * slots * wide, transcendentals=0
         ),
         name="base_rows",
-    )(departure, concentration, departure_class[:, None], shift_ops, carried)
-
-
-MESH = pl.DeviceIdType.MESH
+    )(departure, concentration, departure_class[:, None], shift_ops, carried, own)
+
+
+def shift_of(turn, n):
+    half = lax.div(turn + 1, 2)
+    return lax.rem(n // 2 + n + jnp.where(lax.rem(turn, 2) == 1, half, -half), n)
+
+
+def turn_of(shift, n):
+    apart = lax.rem(shift + n - n // 2, n)
+    return jnp.where(apart == 0, 0, jnp.where(apart <= n // 2, 2 * apart - 1, 2 * (n - apart)))
 
 
 def return_kernel(
@@ -232,7 +256,7 @@
             dst_ref=adv_ref.at[landing],
             send_sem=send_sem.at[turn],
             recv_sem=recv_sem.at[turn],
-            device_id=(lax.rem(me + turn, n),),
+            device_id=(lax.rem(me + shift_of(turn, n), n),),
             device_id_type=MESH,
         )
 
@@ -245,7 +269,7 @@
         )
         speeds = jnp.dot(sent.astype(jnp.bfloat16), spread_low[...], preferred_element_type=jnp.float32)
         base = jnp.concatenate(
-            [got_ref[lax.rem(me + step * group + j, n)] for j in range(group)], axis=0
+            [got_ref[lax.rem(me + shift_of(step * group + j, n), n)] for j in range(group)], axis=0
         )
         values = jnp.dot(base, values_op[...], preferred_element_type=jnp.float32)
         correction = speeds[:, :nodes] * values[:, nodes : 2 * nodes]
@@ -256,18 +280,18 @@
         for j in range(group):
             result[step * group + j] = final[j * capacity : (j + 1) * capacity]
         for j in range(group):
-            if j:
+            if j < group - 1:
                 copy(step * group + j, me).start()
             else:
-                @pl.when(step > 0)
+                @pl.when(step < n // group - 1)
                 def _():
-                    copy(step * group, me).start()
-
-    adv_ref[me] = result[0]
-
-    @pl.loop(1, n)
+                    copy(step * group + group - 1, me).start()
+
+    adv_ref[me] = result[n - 1]
+
+    @pl.loop(0, n - 1)
     def _(turn):
-        copy(turn, lax.rem(me - turn + n, n)).wait()
+        copy(turn, lax.rem(me - shift_of(turn, n) + n, n)).wait()
 
 
 def advect_return(slot, alive, near, far, got, eval_ops):
@@ -296,7 +320,7 @@
             pltpu.SemaphoreType.DMA((n,)),
         ],
         compiler_params=pltpu.CompilerParams(
-            collective_id=0, has_side_effects=True, vmem_limit_bytes=48 * 1024 * 1024
+            collective_id=0, has_side_effects=True, vmem_limit_bytes=24 * 1024 * 1024
         ),
         cost_estimate=pl.CostEstimate(
             flops=2 * n * capacity * (leaves * padded + padded * 3 * nodes + wide * columns),
@@ -341,9 +365,6 @@
     alive = vel_mask.astype(jnp.float32)
     live_density = (density.astype(jnp.float32) * alive[:, None]).astype(jnp.bfloat16)
     wide = jnp.pad(live_density, ((0, 0), (0, 2 * LANES - coef_width)))
-    low, high = halo(wide)
-    local_rows = near_list - my_index * leaves + leaves
-    nearby_field = near_field(low, wide, high, local_rows, near_ops)
     parts = jnp.einsum(
         "gop,opq->goq",
         live_density.reshape(-1, 8, coef_width),
@@ -360,7 +381,9 @@
         carried.reshape(capacity, 3 * columns),
         ((0, 0), (coef_width, 2 * LANES - coef_width - 3 * columns)),
     )
-    base = base_rows(concentration, departure, departure_class, shift_ops, carried)
+    base, low, high = base_rows(concentration, departure, departure_class, shift_ops, carried, wide)
+    local_rows = near_list - my_index * leaves + leaves
+    nearby_field = near_field(low, wide, high, local_rows, near_ops)
     got = lax.all_to_all(
         base.reshape(devices, capacity, -1), "leaf", split_axis=0, concat_axis=0, tiled=True
     )
@@ -389,7 +412,7 @@
     before = jnp.dot(earlier, onehot.astype(jnp.bfloat16), preferred_element_type=jnp.float32)
     rank = jnp.sum(jnp.where(onehot, before, 0.0), axis=1).astype(jnp.int32)
     relative = lax.rem(owner - my_index + devices, devices)
-    send_slot = jnp.where(vel_mask > 0, relative * capacity + rank, -1)
+    send_slot = jnp.where(vel_mask > 0, turn_of(relative, devices) * capacity + rank, -1)
     velocity, advected = advect_return(
         send_slot[None, :], alive[None, :], nearby_field, far, got, eval_ops
     )

time: 114 us -> 123 us (1.079)
  the two profiles are of different devices: /device:TPU:15 before, /device:TPU:0 now
where the time goes in v3:
time: 123 us; the launch traced here: 122 us
  Pallas kernels  90.6 us (74%)
  local copies, waits for them, and re-layouts  18.5 us (15%)
  starting transfers between devices  7.47 us (6%)
  matrix products  2.98 us (2%)
  other arithmetic  1.77 us (1%)
    pallas_call x1, Pallas kernels, near_field(): pl.pallas_call(functools.partial(near_kernel, rows, group), out_shape=jax...  44.5 us
    pallas_call x1, Pallas kernels, advect_return(): pl.pallas_call(functools.partial(return_kernel, n, group), out_shape=(jax...  30.3 us
    unnamed x41, local copies, waits for them, and re-layouts  16.6 us
    pallas_call x1, Pallas kernels, base_rows(): pl.pallas_call(functools.partial(base_kernel, rows, slots // capacity), o...  15.7 us
    all_to_all x1, starting transfers between devices, local(): lax.all_to_all(base.reshape(devices, capacity, -1), 'leaf', split_axis=0,...  7.47 us
  transfers between devices with their start and end apart: 1, of which 0 were waited for; matrix products, arithmetic and copies ran while one was open for 0% of the time, Pallas kernels for 36%

profile of v3, /device:TPU:0, one launch (start us, length us, event | category | flops | bytes accessed | tf_op | source)
XLA Modules:
  0.0 122.2 jit_solution(4837142339165407636)
XLA Ops:
  0.7 1.4 %fusion.2 = f32[1024]{0:T(1024)S(1)} fusion(s32[1024]{0:T(1024)} %bitcast.54), kind=kOutput, calls=%fused_computation.3 | convolution fusion | flops 68287488 | bytes 8192 | tf_op jit(solution)/shard_map/dot_general | solution.py:412
  2.1 1.2 %copy.47 = bf16[1024,220]{1,0:T(8,128)(2,1)S(1)} copy(bf16[1024,220]{0,1:T(8,128)(2,1)} %param.14) | data formatting | bytes 901120 | tf_op args[0]
  3.3 0.8 fusion.21
  4.5 0.4 fusion.3
  5.1 0.9 pad.14.wide_ref.mid_ref
  6.3 0.5 copy.50.field_ref
  6.8 0.4 copy.51.class_ref
  7.2 1.0 copy-done.1
  8.2 15.7 %base_rows.1 = (bf16[2048,256]{1,0:T(8,128)(2,1)}, bf16[1024,256]{1,0:T(8,128)(2,1)S(1)}, bf16[1024,256]{1,0:T(8,128)(2,1)S(1)}) custom-call(s32[2048]{0:T(1024)S(1)} %copy-done.5, bf16[2048,220]{1,0:T(8,128)(2,1)S(1)} %copy.50.field_ref, s32[2048,1]{1,0:T(8,128)S(1)} %copy.51.class_ref, bf16[8,220,220]{2,1,0:T(8,128)(2,1)S(1)} %copy.52.ops_ref, ...), custom_call_target="tpu_custom_call" | custom-call | flops 2147483648 | bytes 2097152 | tf_op jit(solution)/shard_map/base_rows/pallas_call | solution.py:184
  23.9 0.8 copy-done.6
  24.7 0.8 copy-done.8
  25.5 7.5 %all-to-all-start = ((bf16[32,64,256]{2,1,0:T(8,128)(2,1)}), bf16[32,64,256]{2,1,0:T(8,128)(2,1)S(1)}, u32[]{:S(2)}, u32[]{:S(2)}) async-start(bf16[32,64,256]{2,1,0:T(8,128)(2,1)} %bitcast.13), calls=%async_computation | async-start | bytes 2097152 | tf_op jit(solution)/shard_map/all_to_all | solution.py:387
  33.1 1.0 copy-done.2
  34.1 3.6 %copy-done.3 = bf16[27,220,660]{1,2,0:T(8,128)(2,1)S(1)} copy-done((bf16[27,220,660]{1,2,0:T(8,128)(2,1)S(1)}, bf16[27,220,660]{1,2,0:T(8,128)(2,1)}, u32[]{:S(2)}) %copy-start.3) | copy-done | bytes 7840824
  37.7 1.0 copy-done.7
  38.8 1.0 copy-done.9
  39.8 44.5 %near_field.1.near_ref = f32[660,1024]{1,0:T(8,128)S(1)} custom-call(s32[27648]{0:T(1024)S(1)} %reshape.31.idx_ref, bf16[1024,256]{1,0:T(8,128)(2,1)S(1)} %copy-done.7, bf16[1024,256]{1,0:T(8,128)(2,1)S(1)} %copy-done.2, bf16[1024,256]{1,0:T(8,128)(2,1)S(1)} %copy-done.9, bf16[27,660,220]{2,1,0:T(8,128)(2,1)S(1)} %bitcast.51), custom_call_target="tpu_custom_call" | custom-call | flops 46714060800 | bytes 100000000 | tf_op jit(solution)/shard_map/near_field/pallas_call | solution.py:95
  84.4 1.5 %copy-done.10 = f32[660,1024]{1,0:T(8,128)} copy-done((f32[660,1024]{1,0:T(8,128)}, f32[660,1024]{1,0:T(8,128)S(1)}, u32[]{:S(2)}) %copy-start.10) | copy-done | bytes 2703384
  85.9 0.5 convert_reduce_fusion
  86.7 0.8 fusion.6
  88.0 1.8 %copy-done.11 = f32[660,1024]{1,0:T(8,128)S(1)} copy-done((f32[660,1024]{1,0:T(8,128)S(1)}, f32[660,1024]{1,0:T(8,128)}, u32[]{:S(2)}) %copy-start.11) | copy-done | bytes 2703384
  89.8 30.3 %advect_return.1 = (bf16[660,1024]{1,0:T(8,128)(2,1)S(1)}, bf16[32,64,256]{2,1,0:T(8,128)(2,1)S(1)}) custom-call(s32[1,1024]{1,0:T(1,128)S(1)} %bitcast.50, f32[1,1024]{1,0:T(1,128)S(1)} %bitcast.49, f32[660,1024]{1,0:T(8,128)S(1)} %copy-done.11, f32[660,128]{1,0:T(8,128)S(1)} %copy.54.far_ref, bf16[32,64,256]{2,1,0:T(8,128)(2,1)S(1)} %all-to-all-done.got_ref, ...), custom_call_target="tpu_custom_call" | custom-call | flops 6710886400 | bytes 10000000 | tf_op jit(solution)/shard_map/advect_return/pallas_call | solution.py:305
  120.2 1.1 copy.68
  121.2 1.0 copy.69
  (44 shorter events, 1.6 us)
Async XLA Ops:
  0.6 86.9 %copy-start = (bf16[8,56,220]{2,1,0:T(8,128)(2,1)S(1)}, bf16[8,56,220]{2,1,0:T(8,128)(2,1)}, u32[]{:S(2)}) copy-start(bf16[8,56,220]{2,1,0:T(8,128)(2,1)} %param.21) | copy-start | bytes 591364
  0.6 3.9 %copy-start.17 = (bf16[8,220,56]{1,2,0:T(8,128)(2,1)S(1)}, bf16[8,220,56]{1,2,0:T(8,128)(2,1)}, u32[]{:S(2)}) copy-start(bf16[8,220,56]{1,2,0:T(8,128)(2,1)} %param.18) | copy-start | bytes 591364
  0.7 5.4 %copy-start.13 = (bf16[8,220,220]{2,0,1:T(8,128)(2,1)S(1)}, bf16[8,220,220]{2,0,1:T(8,128)(2,1)}, u32[]{:S(2)}) copy-start(bf16[8,220,220]{2,0,1:T(8,128)(2,1)} %param.26) | copy-start | bytes 2323204
  0.7 5.6 %copy-start.12 = (bf16[2048,220]{0,1:T(8,128)(2,1)S(1)}, bf16[2048,220]{0,1:T(8,128)(2,1)}, u32[]{:S(2)}) copy-start(bf16[2048,220]{0,1:T(8,128)(2,1)} %param.23) | copy-start | bytes 2703364
  2.1 4.7 %copy-start.16 = (s32[2048]{0:T(1024)S(1)}, s32[2048]{0:T(1024)}, u32[]{:S(2)}) copy-start(s32[2048]{0:T(1024)} %param.25) | copy-start | bytes 24580
  4.1 3.1 %copy-start.5 = (s32[2048]{0:T(1024)S(1)}, s32[2048]{0:T(1024)}, u32[]{:S(2)}) copy-start(s32[2048]{0:T(1024)} %idx_ref.1) | copy-start | bytes 24580
  7.2 1.0 copy-start.1
  8.2 24.8 %copy-start.14 = (s32[1024,27]{0,1:T(8,128)S(1)}, s32[1024,27]{0,1:T(8,128)}, u32[]{:S(2)}) copy-start(s32[1024,27]{0,1:T(8,128)} %param.16) | copy-start | bytes 331780
  23.9 0.8 copy-start.6
  24.7 0.8 copy-start.8
  25.5 60.3 %all-to-all-start = ((bf16[32,64,256]{2,1,0:T(8,128)(2,1)}), bf16[32,64,256]{2,1,0:T(8,128)(2,1)S(1)}, u32[]{:S(2)}, u32[]{:S(2)}) async-start(bf16[32,64,256]{2,1,0:T(8,128)(2,1)} %bitcast.13), calls=%async_computation | async-start | bytes 2097152 | tf_op jit(solution)/shard_map/all_to_all | solution.py:387
  33.1 1.0 copy-start.2
  34.1 3.6 %copy-start.3 = (bf16[27,220,660]{1,2,0:T(8,128)(2,1)S(1)}, bf16[27,220,660]{1,2,0:T(8,128)(2,1)}, u32[]{:S(2)}) copy-start(bf16[27,220,660]{1,2,0:T(8,128)(2,1)} %param.17) | copy-start | bytes 23522404
  37.7 1.0 copy-start.7
  38.8 1.0 copy-start.9
  39.8 46.6 %copy-start.15 = (f32[56,168]{1,0:T(8,128)S(1)}, f32[56,168]{1,0:T(8,128)}, u32[]{:S(2)}) copy-start(f32[56,168]{1,0:T(8,128)} %param.19) | copy-start | bytes 112900
  39.8 48.2 %copy-start.4 = (bf16[220,1024]{1,0:T(8,128)(2,1)S(1)}, bf16[220,1024]{1,0:T(8,128)(2,1)}, u32[]{:S(2)}) copy-start(bf16[220,1024]{1,0:T(8,128)(2,1)} %eval_ref.1) | copy-start | bytes 1351684
  84.3 1.5 %copy-start.10 = (f32[660,1024]{1,0:T(8,128)}, f32[660,1024]{1,0:T(8,128)S(1)}, u32[]{:S(2)}) copy-start(f32[660,1024]{1,0:T(8,128)S(1)} %near_field.1.near_ref) | copy-start | bytes 8110084
  88.0 1.8 %copy-start.11 = (f32[660,1024]{1,0:T(8,128)S(1)}, f32[660,1024]{1,0:T(8,128)}, u32[]{:S(2)}) copy-start(f32[660,1024]{1,0:T(8,128)} %copy-done.10) | copy-start | bytes 8110084

commit v4 on v2

--- a/solution.py
+++ b/solution.py
@@ -23,36 +23,58 @@
     return lax.ppermute(block, "leaf", forward), lax.ppermute(block, "leaf", backward)
 
 
-def lane_halves(target, at, values):
+MARGIN = 8
+
+
+def lane_halves(low, high, at, values):
     count, width = values.shape
-    target[pl.ds(at, count, stride=2), :] = values[:, :LANES]
+    low[pl.ds(at, count), :] = values[:, :LANES]
     upper = values[:, LANES:]
     if width < 2 * LANES:
         upper = jnp.concatenate([upper, jnp.zeros((count, 2 * LANES - width), values.dtype)], axis=1)
-    target[pl.ds(at + 1, count, stride=2), :] = upper
-
-
-def near_kernel(rows, group, idx_ref, low_ref, mid_ref, high_ref, ops_ref, out_ref, source, picked, lhs, raw, weights, sem):
+    high[pl.ds(at, count), :] = upper
+
+
+def starts_of(rows):
+    spread = jnp.arange(rows.shape[-1], dtype=jnp.int32) % MARGIN
+    return rows + (MARGIN - spread)
+
+
+def gather_groups(sources, starts_ref, at, rows):
+    sublane = lax.broadcasted_iota(jnp.int32, (MARGIN, LANES), 0)
+    bits = [lax.rem(lax.div(sublane, 1 << bit), 2) == 1 for bit in range(3)]
+    for first in range(0, rows, 2 * MARGIN):
+        parts = [[], []]
+        for group in range(first, first + 2 * MARGIN, MARGIN):
+            starts = [starts_ref[at + group + k] for k in range(MARGIN)]
+            for part, source in zip(parts, sources):
+                loads = [source[pl.ds(start, MARGIN), :] for start in starts]
+                for bit in bits:
+                    loads = [jnp.where(bit, b, a) for a, b in zip(loads[::2], loads[1::2])]
+                part.append(loads[0])
+        yield first, [jnp.concatenate(part, axis=0) for part in parts]
+
+
+def near_kernel(
+    rows, group, idx_ref, low_ref, mid_ref, high_ref, ops_ref, out_ref,
+    source_low, source_high, lhs_even, lhs_odd, raw, weights, sem,
+):
     block = pl.program_id(0)
     taps, _, depth = ops_ref.shape
     wide = 2 * LANES
     leaves = mid_ref.shape[0]
+    turns = taps // group
     fetch = pltpu.make_async_copy(ops_ref, raw, sem)
 
-    def pick(turn):
+    def pick(turn, lhs):
         for j in range(group):
             at = (turn * group + j) * leaves + block * rows
-            for r in range(rows):
-                row = pl.multiple_of(idx_ref[at + r], 2)
-                picked[pl.ds(2 * (j * rows + r), 2), :] = source[pl.ds(row, 2), :]
-
-    def settle():
-        for j in range(group):
-            for half in range(2):
-                values = picked[pl.ds(2 * j * rows + half, rows, stride=2), :]
-                lhs[:, (2 * j + half) * LANES : (2 * j + half + 1) * LANES] = values.astype(jnp.bfloat16)
-
-    def product(turn):
+            for first, halves in gather_groups((source_low, source_high), idx_ref, at, rows):
+                for half, values in enumerate(halves):
+                    column = (2 * j + half) * LANES
+                    lhs[first : first + 2 * MARGIN, column : column + LANES] = values.astype(jnp.bfloat16)
+
+    def product(turn, lhs):
         at = pl.multiple_of(turn * (group * wide), group * wide)
         return lax.dot_general(
             weights[:, pl.ds(at, group * wide)],
@@ -68,10 +90,9 @@
             @pl.loop(0, leaves // rows)
             def _(chunk):
                 values = ref[pl.ds(chunk * rows, rows), :].astype(jnp.float32)
-                lane_halves(source, 2 * (part * leaves + chunk * rows), values)
-
-    pick(0)
-    settle()
+                lane_halves(source_low, source_high, MARGIN + part * leaves + chunk * rows, values)
+
+    pick(0, lhs_even)
 
     @pl.when(block == 0)
     def _():
@@ -82,13 +103,20 @@
 
     out_ref[...] = jnp.zeros_like(out_ref)
 
-    @pl.loop(0, taps // group - 1)
-    def _(turn):
-        out_ref[...] += product(turn)
-        pick(turn + 1)
-        settle()
-
-    out_ref[...] += product(taps // group - 1)
+    @pl.loop(0, (turns - 1) // 2)
+    def _(pair):
+        turn = 2 * pair
+        out_ref[...] += product(turn, lhs_even)
+        pick(turn + 1, lhs_odd)
+        out_ref[...] += product(turn + 1, lhs_odd)
+        pick(turn + 2, lhs_even)
+
+    if turns % 2 == 0:
+        out_ref[...] += product(turns - 2, lhs_even)
+        pick(turns - 1, lhs_odd)
+        out_ref[...] += product(turns - 1, lhs_odd)
+    else:
+        out_ref[...] += product(turns - 1, lhs_even)
 
 
 def near_field(low, mid, high, local_rows, near_ops):
@@ -96,7 +124,7 @@
     taps, depth, outs = near_ops.shape
     rows = 256 if leaves % 256 == 0 else leaves
     group = 3 if taps % 3 == 0 else 1
-    flat = (2 * local_rows).T.reshape(-1)
+    flat = starts_of(local_rows.T).reshape(-1)
     vmem = pl.BlockSpec(memory_space=pltpu.VMEM)
     return pl.pallas_call(
         functools.partial(near_kernel, rows, group),
@@ -107,15 +135,16 @@
         ],
         out_specs=pl.BlockSpec((outs, rows), lambda i: (0, i)),
         scratch_shapes=[
-            pltpu.VMEM((6 * leaves, LANES), jnp.float32),
-            pltpu.VMEM((2 * group * rows, LANES), jnp.float32),
+            pltpu.VMEM((3 * leaves + 2 * MARGIN, LANES), jnp.float32),
+            pltpu.VMEM((3 * leaves + 2 * MARGIN, LANES), jnp.float32),
+            pltpu.VMEM((rows, group * 2 * LANES), jnp.bfloat16),
             pltpu.VMEM((rows, group * 2 * LANES), jnp.bfloat16),
             pltpu.VMEM((taps, outs, depth), jnp.bfloat16),
             pltpu.VMEM((outs, taps * 2 * LANES), jnp.bfloat16),
             pltpu.SemaphoreType.DMA(()),
         ],
         compiler_params=pltpu.CompilerParams(
-            dimension_semantics=("arbitrary",), vmem_limit_bytes=48 * 1024 * 1024
+            dimension_semantics=("arbitrary",), vmem_limit_bytes=60 * 1024 * 1024
         ),
         cost_estimate=pl.CostEstimate(
             flops=2 * leaves * taps * 2 * LANES * outs * 5, bytes_accessed=100_000_000, transcendentals=0
@@ -124,7 +153,7 @@
     )(flat, low, mid, high, near_ops.transpose(0, 2, 1))
 
 
-def base_kernel(rows, capacity, idx_ref, field_ref, class_ref, ops_ref, carried_ref, out_ref, source, picked, lhs, weights):
+def base_kernel(rows, capacity, idx_ref, field_ref, class_ref, ops_ref, carried_ref, out_ref, source_low, source_high, lhs, weights):
     block = pl.program_id(0)
     kinds, depth, outs = ops_ref.shape
     wide = 2 * LANES
@@ -134,7 +163,7 @@
         @pl.loop(0, field_ref.shape[0] // rows)
         def _(chunk):
             values = field_ref[pl.ds(chunk * rows, rows), :].astype(jnp.float32)
-            lane_halves(source, 2 * chunk * rows, values)
+            lane_halves(source_low, source_high, MARGIN + chunk * rows, values)
 
         for kind in range(kinds):
             weights[kind * wide : (kind + 1) * wide, LANES:] = jnp.zeros((wide, LANES), weights.dtype)
@@ -142,15 +171,14 @@
                 [ops_ref[kind], jnp.zeros((wide - depth, outs), ops_ref.dtype)], axis=0
             )
 
-    for r in range(rows):
-        row = pl.multiple_of(2 * idx_ref[block * rows + r], 2)
-        picked[2 * r : 2 * r + 2, :] = source[pl.ds(row, 2), :]
-    halves = [picked[pl.ds(half, rows, stride=2), :] for half in range(2)]
-    for kind in range(kinds):
-        chosen = class_ref[...] == kind
-        for half in range(2):
-            at = kind * wide + half * LANES
-            lhs[:, at : at + LANES] = jnp.where(chosen, halves[half], 0.0).astype(jnp.bfloat16)
+    for first, halves in gather_groups((source_low, source_high), idx_ref, block * rows, rows):
+        here = slice(first, first + 2 * MARGIN)
+        classes = class_ref[here, :]
+        for kind in range(kinds):
+            chosen = classes == kind
+            for half, values in enumerate(halves):
+                at = kind * wide + half * LANES
+                lhs[here, at : at + LANES] = jnp.where(chosen, values, 0.0).astype(jnp.bfloat16)
     total = jnp.dot(lhs[...], weights[...], preferred_element_type=jnp.float32)
     extra = carried_ref[...].astype(jnp.float32)
     out_ref[...] = (total + jnp.concatenate([extra] * (rows // capacity), axis=0)).astype(jnp.bfloat16)
@@ -176,8 +204,8 @@
         ],
         out_specs=pl.BlockSpec((rows, wide), lambda i: (i, 0)),
         scratch_shapes=[
-            pltpu.VMEM((2 * slots, LANES), jnp.float32),
-            pltpu.VMEM((2 * rows, LANES), jnp.float32),
+            pltpu.VMEM((slots + 2 * MARGIN, LANES), jnp.float32),
+            pltpu.VMEM((slots + 2 * MARGIN, LANES), jnp.float32),
             pltpu.VMEM((rows, kinds * wide), jnp.bfloat16),
             pltpu.VMEM((kinds * wide, wide), jnp.bfloat16),
         ],
@@ -188,10 +216,20 @@
             flops=2 * slots * kinds * wide * wide, bytes_accessed=4 * slots * wide, transcendentals=0
         ),
         name="base_rows",
-    )(departure, concentration, departure_class[:, None], shift_ops, carried)
+    )(starts_of(departure), concentration, departure_class[:, None], shift_ops, carried)
 
 
 MESH = pl.DeviceIdType.MESH
+
+
+def shift_of(turn, n):
+    half = lax.div(turn + 1, 2)
+    return lax.rem(n // 2 + n + jnp.where(lax.rem(turn, 2) == 1, half, -half), n)
+
+
+def turn_of(shift, n):
+    apart = lax.rem(shift + n - n // 2, n)
+    return jnp.where(apart == 0, 0, jnp.where(apart <= n // 2, 2 * apart - 1, 2 * (n - apart)))
 
 
 def return_kernel(
@@ -232,7 +270,7 @@
             dst_ref=adv_ref.at[landing],
             send_sem=send_sem.at[turn],
             recv_sem=recv_sem.at[turn],
-            device_id=(lax.rem(me + turn, n),),
+            device_id=(lax.rem(me + shift_of(turn, n), n),),
             device_id_type=MESH,
         )
 
@@ -245,7 +283,7 @@
         )
         speeds = jnp.dot(sent.astype(jnp.bfloat16), spread_low[...], preferred_element_type=jnp.float32)
         base = jnp.concatenate(
-            [got_ref[lax.rem(me + step * group + j, n)] for j in range(group)], axis=0
+            [got_ref[lax.rem(me + shift_of(step * group + j, n), n)] for j in range(group)], axis=0
         )
         values = jnp.dot(base, values_op[...], preferred_element_type=jnp.float32)
         correction = speeds[:, :nodes] * values[:, nodes : 2 * nodes]
@@ -256,18 +294,18 @@
         for j in range(group):
             result[step * group + j] = final[j * capacity : (j + 1) * capacity]
         for j in range(group):
-            if j:
+            if j < group - 1:
                 copy(step * group + j, me).start()
             else:
-                @pl.when(step > 0)
+                @pl.when(step < n // group - 1)
                 def _():
-                    copy(step * group, me).start()
-
-    adv_ref[me] = result[0]
-
-    @pl.loop(1, n)
+                    copy(step * group + group - 1, me).start()
+
+    adv_ref[me] = result[n - 1]
+
+    @pl.loop(0, n - 1)
     def _(turn):
-        copy(turn, lax.rem(me - turn + n, n)).wait()
+        copy(turn, lax.rem(me - shift_of(turn, n) + n, n)).wait()
 
 
 def advect_return(slot, alive, near, far, got, eval_ops):
@@ -389,7 +427,7 @@
     before = jnp.dot(earlier, onehot.astype(jnp.bfloat16), preferred_element_type=jnp.float32)
     rank = jnp.sum(jnp.where(onehot, before, 0.0), axis=1).astype(jnp.int32)
     relative = lax.rem(owner - my_index + devices, devices)
-    send_slot = jnp.where(vel_mask > 0, relative * capacity + rank, -1)
+    send_slot = jnp.where(vel_mask > 0, turn_of(relative, devices) * capacity + rank, -1)
     velocity, advected = advect_return(
         send_slot[None, :], alive[None, :], nearby_field, far, got, eval_ops
     )

time: 114 us -> 115 us (level)
  the two profiles are of different devices: /device:TPU:15 before, /device:TPU:0 now
where the time goes in v4:
time: 115 us; the launch traced here: 114 us
  Pallas kernels  88.2 us (77%)
  starting transfers between devices  12.9 us (11%)
  local copies, waits for them, and re-layouts  7.65 us (7%)
  matrix products  2.93 us (3%)
  other arithmetic  1.79 us (2%)
    pallas_call x1, Pallas kernels, near_field(): pl.pallas_call(functools.partial(near_kernel, rows, group), out_shape=jax...  47.9 us
    pallas_call x1, Pallas kernels, advect_return(): pl.pallas_call(functools.partial(return_kernel, n, group), out_shape=(jax...  32.1 us
    all_to_all x1, starting transfers between devices, local(): lax.all_to_all(base.reshape(devices, capacity, -1), 'leaf', split_axis=0,...  8.43 us
    pallas_call x1, Pallas kernels, base_rows(): pl.pallas_call(functools.partial(base_kernel, rows, capacity), out_shape=...  8.28 us
    unnamed x21, local copies, waits for them, and re-layouts  5.18 us
    ppermute x1, starting transfers between devices, halo(): lax.ppermute(block, 'leaf', forward)  3.16 us
  transfers between devices with their start and end apart: 3, of which 0 were waited for; matrix products, arithmetic and copies ran while one was open for 3% of the time, Pallas kernels for 49%

profile of v4, /device:TPU:0, one launch (start us, length us, event | category | flops | bytes accessed | tf_op | source)
XLA Modules:
  0.0 114.4 jit_solution(8023193554097571185)
XLA Ops:
  0.7 1.3 %fusion.2 = f32[1024]{0:T(1024)S(1)} fusion(s32[1024]{0:T(1024)} %bitcast.53), kind=kOutput, calls=%fused_computation.3 | convolution fusion | flops 68287488 | bytes 8192 | tf_op jit(solution)/shard_map/dot_general | solution.py:427
  2.0 1.2 %copy.47 = bf16[1024,220]{1,0:T(8,128)(2,1)S(1)} copy(bf16[1024,220]{0,1:T(8,128)(2,1)} %param.14) | data formatting | bytes 901120 | tf_op args[0]
  3.3 0.8 fusion.30
  4.0 0.2 multiply_convert_fusion
  4.3 0.9 pad.12.mid_ref
  5.1 3.2 %collective-permute-start = (bf16[1024,256]{1,0:T(8,128)(2,1)}, bf16[1024,256]{1,0:T(8,128)(2,1)}, u32[]{:S(2)}, u32[]{:S(2)}) collective-permute-start(bf16[1024,256]{1,0:T(8,128)(2,1)} %pad.12.mid_ref), channel_id=1, source_target_pairs={{0,1},{1,2},{2,3},{3,4},{4,5},{5,6},{6,7},{7,8},{8,9},{9,10},{10,1... | collective-permute-start | bytes 1572872 | tf_op jit(solution)/shard_map/ppermute | solution.py:23
  8.3 1.3 %collective-permute-start.1 = (bf16[1024,256]{1,0:T(8,128)(2,1)}, bf16[1024,256]{1,0:T(8,128)(2,1)}, u32[]{:S(2)}, u32[]{:S(2)}) collective-permute-start(bf16[1024,256]{1,0:T(8,128)(2,1)} %pad.12.mid_ref), channel_id=1, source_target_pairs={{1,0},{2,1},{3,2},{4,3},{5,4},{6,5},{7,6},{8,7},{9,8},{10,9},{11,1... | collective-permute-start | bytes 1572872 | tf_op jit(solution)/shard_map/ppermute | solution.py:23
  9.6 0.2 fusion.35
  9.8 0.4 fusion.3
  10.5 0.5 copy.50.field_ref
  11.0 0.4 copy.51.class_ref
  11.4 1.4 %copy.52.ops_ref = bf16[8,220,220]{2,1,0:T(8,128)(2,1)S(1)} copy(bf16[8,220,220]{2,0,1:T(8,128)(2,1)} %param.26) | data formatting | bytes 1548800 | tf_op args[12]
  12.8 8.3 %base_rows.1 = bf16[2048,256]{1,0:T(8,128)(2,1)} custom-call(s32[2048]{0:T(1024)S(1)} %fusion.9.idx_ref, bf16[2048,220]{1,0:T(8,128)(2,1)S(1)} %copy.50.field_ref, s32[2048,1]{1,0:T(8,128)S(1)} %copy.51.class_ref, bf16[8,220,220]{2,1,0:T(8,128)(2,1)S(1)} %copy.52.ops_ref, bf16[64,256]{1,0:T(8,128)(2,1)S(1)} %pad.14.carried_ref), custom_call_target="tpu_custom_call" | custom-call | flops 2147483648 | bytes 2097152 | tf_op jit(solution)/shard_map/base_rows/pallas_call | solution.py:194
  21.0 8.4 %all-to-all-start = ((bf16[32,64,256]{2,1,0:T(8,128)(2,1)}), bf16[32,64,256]{2,1,0:T(8,128)(2,1)S(1)}, u32[]{:S(2)}, u32[]{:S(2)}) async-start(bf16[32,64,256]{2,1,0:T(8,128)(2,1)} %bitcast.13), calls=%async_computation | async-start | bytes 2097152 | tf_op jit(solution)/shard_map/all_to_all | solution.py:402
  29.5 0.7 reshape.41.idx_ref
  30.2 47.9 %near_field.1.near_ref = f32[660,1024]{1,0:T(8,128)} custom-call(s32[27648]{0:T(1024)} %reshape.41.idx_ref, bf16[1024,256]{1,0:T(8,128)(2,1)} %collective-permute-done.low_ref, bf16[1024,256]{1,0:T(8,128)(2,1)} %pad.12.mid_ref, bf16[1024,256]{1,0:T(8,128)(2,1)} %collective-permute-done.1.high_ref, bf16[27,660,220]{2,1,0:T(8,128)(2,1)} %bitcast.55), custom_call_target="tpu_custom_call" | custom-call | flops 46714060800 | bytes 100000000 | tf_op jit(solution)/shard_map/near_field/pallas_call | solution.py:129
  78.1 0.5 convert_reduce_fusion
  78.7 0.1 convolution_bitcast_fusion.2
  78.9 0.8 fusion.6
  79.7 0.2 convolution_bitcast_fusion
  80.1 0.2 copy.54.far_ref
  80.2 32.1 %advect_return.1 = (bf16[660,1024]{1,0:T(8,128)(2,1)S(1)}, bf16[32,64,256]{2,1,0:T(8,128)(2,1)S(1)}) custom-call(s32[1,1024]{1,0:T(1,128)S(1)} %bitcast.50, f32[1,1024]{1,0:T(1,128)S(1)} %bitcast.49, f32[660,1024]{1,0:T(8,128)} %near_field.1.near_ref, f32[660,128]{1,0:T(8,128)S(1)} %copy.54.far_ref, bf16[32,64,256]{2,1,0:T(8,128)(2,1)S(1)} %all-to-all-done.got_ref, ...), custom_call_target="tpu_custom_call" | custom-call | flops 6710886400 | bytes 10000000 | tf_op jit(solution)/shard_map/advect_return/pallas_call | solution.py:319
  112.3 1.1 copy.68
  113.4 1.0 copy.69
  (30 shorter events, 0.5 us)
Async XLA Ops:
  0.6 79.1 %copy-start = (bf16[8,56,220]{2,1,0:T(8,128)(2,1)S(1)}, bf16[8,56,220]{2,1,0:T(8,128)(2,1)}, u32[]{:S(2)}) copy-start(bf16[8,56,220]{2,1,0:T(8,128)(2,1)} %param.21) | copy-start | bytes 591364
  0.6 9.2 %copy-start.7 = (bf16[8,220,56]{1,2,0:T(8,128)(2,1)S(1)}, bf16[8,220,56]{1,2,0:T(8,128)(2,1)}, u32[]{:S(2)}) copy-start(bf16[8,220,56]{1,2,0:T(8,128)(2,1)} %param.18) | copy-start | bytes 591364
  0.7 9.8 %copy-start.2 = (bf16[2048,220]{0,1:T(8,128)(2,1)S(1)}, bf16[2048,220]{0,1:T(8,128)(2,1)}, u32[]{:S(2)}) copy-start(bf16[2048,220]{0,1:T(8,128)(2,1)} %param.23) | copy-start | bytes 2703364
  0.7 10.3 %copy-start.5 = (s32[2048]{0:T(1024)S(1)}, s32[2048]{0:T(1024)}, u32[]{:S(2)}) copy-start(s32[2048]{0:T(1024)} %param.25) | copy-start | bytes 24580
  4.0 8.7 %copy-start.6 = (s32[2048]{0:T(1024)S(1)}, s32[2048]{0:T(1024)}, u32[]{:S(2)}) copy-start(s32[2048]{0:T(1024)} %param.24) | copy-start | bytes 24580
  5.1 25.1 %collective-permute-start = (bf16[1024,256]{1,0:T(8,128)(2,1)}, bf16[1024,256]{1,0:T(8,128)(2,1)}, u32[]{:S(2)}, u32[]{:S(2)}) collective-permute-start(bf16[1024,256]{1,0:T(8,128)(2,1)} %pad.12.mid_ref), channel_id=1, source_target_pairs={{0,1},{1,2},{2,3},{3,4},{4,5},{5,6},{6,7},{7,8},{8,9},{9,10},{10,1... | collective-permute-start | bytes 1572872 | tf_op jit(solution)/shard_map/ppermute | solution.py:23
  8.3 21.9 %collective-permute-start.1 = (bf16[1024,256]{1,0:T(8,128)(2,1)}, bf16[1024,256]{1,0:T(8,128)(2,1)}, u32[]{:S(2)}, u32[]{:S(2)}) collective-permute-start(bf16[1024,256]{1,0:T(8,128)(2,1)} %pad.12.mid_ref), channel_id=1, source_target_pairs={{1,0},{2,1},{3,2},{4,3},{5,4},{6,5},{7,6},{8,7},{9,8},{10,9},{11,1... | collective-permute-start | bytes 1572872 | tf_op jit(solution)/shard_map/ppermute | solution.py:23
  12.7 16.8 %copy-start.3 = (s32[1024,27]{0,1:T(8,128)S(1)}, s32[1024,27]{0,1:T(8,128)}, u32[]{:S(2)}) copy-start(s32[1024,27]{0,1:T(8,128)} %param.16) | copy-start | bytes 331780
  21.0 57.1 %all-to-all-start = ((bf16[32,64,256]{2,1,0:T(8,128)(2,1)}), bf16[32,64,256]{2,1,0:T(8,128)(2,1)S(1)}, u32[]{:S(2)}, u32[]{:S(2)}) async-start(bf16[32,64,256]{2,1,0:T(8,128)(2,1)} %bitcast.13), calls=%async_computation | async-start | bytes 2097152 | tf_op jit(solution)/shard_map/all_to_all | solution.py:402
  30.2 48.4 %copy-start.4 = (f32[56,168]{1,0:T(8,128)S(1)}, f32[56,168]{1,0:T(8,128)}, u32[]{:S(2)}) copy-start(f32[56,168]{1,0:T(8,128)} %param.19) | copy-start | bytes 112900
  30.2 50.0 %copy-start.1 = (bf16[220,1024]{1,0:T(8,128)(2,1)S(1)}, bf16[220,1024]{1,0:T(8,128)(2,1)}, u32[]{:S(2)}) copy-start(bf16[220,1024]{1,0:T(8,128)(2,1)} %eval_ref.1) | copy-start | bytes 1351684
